TPU v7x, 512 devices: a whole 4x4x16 slice. The times are simulated.
512 devices in a mesh: dp: 64 (over z, y), mp: 8 (over x, core).
Axes of the slice: x: 4, y: 4, z: 16, core: 2. Of those that a mesh axis runs over, the one named last changes fastest.
Arguments:
- query_raw: bfloat16 [8192, 1024], P('dp', 'mp'), may hold values from -4 to 4
- key_raw: bfloat16 [8192, 1024], P('dp', 'mp'), may hold values from -4 to 4
- values: bfloat16 [8192, 2048], P('dp', 'mp'), may hold values from -8 to 8
- decay_input: float32 [8192, 16], P('dp', 'mp'), may hold values from -4 to 4
- beta_input: float32 [8192, 16], P('dp', 'mp'), may hold values from -6 to 6
- log_rate: float32 [16], P('mp'), may hold values from -3 to 1
- step_bias: float32 [16], P('mp'), may hold values from -2 to 1
- gain: float32 [128], replicated, may hold values from 0.5 to 1.5
- out_weight: bfloat16 [2048, 2048], P('mp'), may hold values from -0.125 to 0.125
- upstream: bfloat16 [8192, 2048], P('dp'), may hold values from -0.1875 to 0.1875
Outputs:
- weight_grad: bfloat16 [2048, 2048], P('mp')
- gain_grad: float32 [128], replicated
- decay_grad: float32 [16], replicated
All inputs are finite; a program needn't handle non-finite values.
Results may differ from a plain program's by a relative error of at most 0.0033.
Values may be sent and summed in bfloat16 or wider, within the bound.
No kernel may reach another device: no remote copies, remote signals or barrier semaphores. Data moves between devices by JAX's collectives and lax.ppermute only.
A program may use at most 64 MiB of HBM per device.

v0:
```python
import jax
import jax.numpy as jnp
from jax import lax
from jax.sharding import PartitionSpec as P

SPAN = 64


EPS = 1e-06
HIGH = lax.Precision.HIGHEST


def from_partner(value, axis, apart):
    mask = 2**apart
    pairs = [(source, source ^ mask) for source in range(lax.axis_size(axis))]
    return lax.ppermute(value, axis, pairs)


def unit_rows(raw, heads):
    count = raw.shape[0]
    shaped = raw.astype(jnp.float32).reshape(count, heads, -1)
    return shaped / jnp.sqrt(jnp.sum(shaped * shaped, axis=-1, keepdims=True) + EPS)


def span_step(state, block):
    query, keys, vals, log_decay, beta = block
    width = query.shape[-1]
    count = log_decay.shape[-1]
    places = jnp.arange(count)
    lower = places[:, None] >= places[None, :]
    strict = places[:, None] > places[None, :]
    cumul = jnp.cumsum(log_decay, axis=1)
    spread = cumul[:, :, None] - cumul[:, None, :]
    decay = jnp.where(lower, jnp.exp(jnp.where(lower, spread, 0.0)), 0.0)
    inner = jnp.einsum("hid,hjd->hij", keys, keys, precision=HIGH)
    coupling = jnp.where(strict, beta[:, :, None] * inner * decay, 0.0)
    system = coupling + jnp.eye(count, dtype=log_decay.dtype)
    growth = jnp.exp(cumul)
    right = jnp.concatenate([beta[:, :, None] * vals, (beta * growth)[:, :, None] * keys], axis=2)
    solved = jax.scipy.linalg.solve_triangular(system, right, lower=True, unit_diagonal=True)
    writes = solved[:, :, :width] - jnp.einsum(
        "hcd,hde->hce", solved[:, :, width:], state, precision=HIGH
    )
    scores = jnp.einsum("hid,hjd->hij", query, keys, precision=HIGH) * decay
    output = growth[:, :, None] * jnp.einsum("hcd,hde->hce", query, state, precision=HIGH)
    output = output + jnp.einsum("hij,hje->hie", scores, writes, precision=HIGH)
    final = cumul[:, -1]
    weighted = keys * jnp.exp(final[:, None] - cumul)[:, :, None]
    carried = jnp.exp(final)[:, None, None] * state + jnp.einsum(
        "hcd,hce->hde", weighted, writes, precision=HIGH
    )
    return (carried, output)


def delta_rule(query, keys, vals, log_decay, beta):
    count, heads, width = vals.shape
    blocks = count // SPAN

    def split(array):
        shaped = array.reshape((blocks, SPAN) + array.shape[1:])
        return jnp.swapaxes(shaped, 1, 2)

    start = jnp.zeros((heads, width, width), vals.dtype)
    ending, outputs = lax.scan(
        span_step, start, (split(query), split(keys), split(vals), split(log_decay), split(beta))
    )
    return jnp.swapaxes(outputs, 1, 2).reshape(count, heads, width)


def layer_forward(query_raw, key_raw, values, decay_input, beta_input, log_rate, step_bias, gain):
    width = gain.shape[0]
    qk_heads = query_raw.shape[1] // width
    heads = log_rate.shape[0]
    count = values.shape[0]
    repeat = heads // qk_heads
    query = jnp.repeat(unit_rows(query_raw, qk_heads) * width ** (-0.5), repeat, axis=1)
    keys = jnp.repeat(unit_rows(key_raw, qk_heads), repeat, axis=1)
    vals = values.astype(jnp.float32).reshape(count, heads, width)
    log_decay = -jnp.exp(log_rate)[None, :] * jax.nn.softplus(decay_input + step_bias[None, :])
    beta = jax.nn.sigmoid(beta_input)
    mixed = delta_rule(query, keys, vals, log_decay, beta)
    scale = lax.rsqrt(jnp.mean(mixed * mixed, axis=-1, keepdims=True) + EPS)
    return (mixed * scale * gain).reshape(count, heads * width)


def mix_pair(first, second, inner, first_norm, second_norm):
    first_coef = 1.0 - inner / (2.0 * (first_norm + EPS))
    second_coef = 1.0 - inner / (2.0 * (second_norm + EPS))
    return first_coef * first + second_coef * second


def pair_local(first, second):
    return mix_pair(
        first, second, jnp.sum(first * second), jnp.sum(first * first), jnp.sum(second * second)
    )


def local_tree(stack):
    while stack.shape[0] > 1:
        half = stack.shape[0] // 2
        stack = jax.vmap(pair_local)(stack[:half], stack[half:])
    return stack[0]


def combine_weights(grad_w):
    levels = lax.axis_size("dp").bit_length() - 1
    position = lax.axis_index("dp")
    current = grad_w
    for level in range(levels):
        bit = levels - 1 - level
        upper = jnp.right_shift(position, bit) % 2 == 1
        half = current.shape[0] // 2
        lower_rows = current[:half]
        upper_rows = current[half:]
        outgoing = jnp.where(upper, lower_rows, upper_rows)
        kept = jnp.where(upper, upper_rows, lower_rows)
        incoming = from_partner(outgoing, "dp", bit)
        first = jnp.where(upper, incoming, kept)
        second = jnp.where(upper, kept, incoming)
        partial_value = jnp.stack(
            [jnp.sum(first * second), jnp.sum(first * first), jnp.sum(second * second)]
        )
        slots = 2**bit
        chosen = jnp.arange(slots, dtype=jnp.int32)[None, :] == position % slots
        table = lax.psum(jnp.where(chosen, partial_value[:, None], 0.0), ("dp", "mp"))
        totals = jnp.sum(jnp.where(chosen, table, 0.0), axis=1)
        current = mix_pair(first, second, totals[0], totals[1], totals[2])
    return current


def combine_small(gain_vec, rate_vec):
    gain_stack, rate_stack = (
        lax.all_gather(gain_vec[None, :], "dp", axis=0, tiled=True),
        lax.all_gather(rate_vec[None, :], "dp", axis=0, tiled=True),
    )
    return (local_tree(gain_stack), local_tree(rate_stack))


def per_device(
    query_raw,
    key_raw,
    values,
    decay_input,
    beta_input,
    log_rate,
    step_bias,
    gain,
    out_weight,
    upstream,
):

    def forward(rates, gains):
        return layer_forward(
            query_raw, key_raw, values, decay_input, beta_input, rates, step_bias, gains
        )

    normed, pull = jax.vjp(forward, log_rate, gain)
    grad_w = lax.dot_general(
        normed.astype(jnp.bfloat16),
        upstream,
        (((0,), (0,)), ((), ())),
        preferred_element_type=jnp.float32,
    )
    own_piece = combine_weights(grad_w)
    d_normed = lax.dot_general(
        upstream, out_weight, (((1,), (1,)), ((), ())), preferred_element_type=jnp.float32
    )
    grad_rate, grad_gain = pull(d_normed)
    mp_count = lax.axis_size("mp")
    heads = log_rate.shape[0]
    placed = lax.dynamic_update_slice(
        jnp.zeros((heads * mp_count,), jnp.float32), grad_rate, (lax.axis_index("mp") * heads,)
    )
    gain_total, rate_total = lax.psum((grad_gain, placed), "mp")
    gain_final, rate_final = combine_small(gain_total, rate_total)
    whole = lax.all_gather(own_piece.astype(jnp.bfloat16), "dp", axis=0, tiled=True)
    return (whole, gain_final, rate_final)


def solution(mesh):
    in_specs = (
        P("dp", "mp"),
        P("dp", "mp"),
        P("dp", "mp"),
        P("dp", "mp"),
        P("dp", "mp"),
        P("mp"),
        P("mp"),
        P(),
        P("mp", None),
        P("dp", None),
    )
    out_specs = (P("mp", None), P(), P())
    return jax.shard_map(
        per_device, mesh=mesh, in_specs=in_specs, out_specs=out_specs, check_vma=False
    )
```

profile of v0, /device:TPU:2, one launch (start us, length us, event | category | flops | bytes accessed | tf_op | source)
XLA Modules:
  0.0 1174.1 jit_solution(3240681862797782701)
XLA Ops:
  12.4 1.3 broadcast_multiply_fusion
  15.4 34.7 %while.67 = (s32[]{:T(128)}, f32[2,128,128]{2,1,0:T(8,128)S(1)}, f32[2,2,64,128]{3,2,1,0:T(8,128)S(1)}, f32[2,2,64,64]{3,2,1,0:T(8,128)}, f32[2,2,64,64]{3,2,1,0...) while((s32[]{:T(128)}, f32[2,128,128]{2,1,0:T(8,128)S(1)}, ...), condition=%wide.region_4.5_spmd.clone.clone, body=%wide.region_2.4_spmd.clone.clone.sunk | while | flops 138965312 | bytes 5778934 | solution.py:64
  16.4 9.8 custom-call.44
  33.8 9.8 custom-call.44
  52.7 1.6 fusion.140
  55.4 15.7 %collective-permute-start = (f32[128,2048]{1,0:T(8,128)}, f32[128,2048]{1,0:T(8,128)}, u32[]{:S(2)}, u32[]{:S(2)}) collective-permute-start(f32[128,2048]{1,0:T(8,128)} %slice_select_fusion.1), channel_id=1, source_target_pairs={{0,256},{8,264},{16,272},{24,280},{32,288},{40,296},{48,304},{56,3... | collective-permute-start | bytes 3145736 | tf_op jit(solution)/shard_map/ppermute | solution.py:16
  71.1 1.7 multiply_reduce_fusion.10
  72.8 1.8 fusion.136
  75.8 66.8 %while.68 = (s32[]{:T(128)}, f32[2,128,128]{2,1,0:T(8,128)S(1)}, f32[2,2,64]{2,1,0:T(2,128)}, f32[2,2,1,1]{1,3,2,0:T(1,128)}, f32[2,2,64,128]{3,2,1,0:T(8,128)},...) while((s32[]{:T(128)}, f32[2,128,128]{2,1,0:T(8,128)S(1)}, ...), condition=%wide.region_66.67_spmd.clone.clone, body=%wide.region_57.66_spmd.clone.clone.sunk | while | flops 195670848 | bytes 3316196 | solution.py:64
  79.3 1.8 fusion.248
  81.2 1.5 add_bitcast_fusion.7
  82.7 11.2 custom-call.45
  95.0 1.9 fusion.250
  96.8 1.7 fusion.252
  106.7 1.3 convolution_add_fusion.10
  112.8 1.8 fusion.248
  114.7 1.5 add_bitcast_fusion.7
  116.1 11.2 custom-call.45
  128.4 1.9 fusion.250
  130.3 1.7 fusion.252
  145.8 11.4 all-reduce.3
  157.1 72.6 %all-gather.2 = f32[64,1,16]{2,1,0:T(1,128)S(1)} all-gather(f32[1,1,16]{2,1,0:T(1,128)S(1)} %bitcast.415), channel_id=1, replica_groups=mesh['dp'=64,'mp'=8] {'dp'}, dimensions={0}, use_global_device_ids=true | all-gather | bytes 4160 | tf_op jit(solution)/shard_map/all_gather | solution.py:134
  230.7 71.5 %all-gather.1 = f32[64,1,128]{2,1,0:T(1,128)S(1)} all-gather(f32[1,1,128]{2,1,0:T(1,128)S(1)} %bitcast.414), channel_id=1, replica_groups=mesh['dp'=64,'mp'=8] {'dp'}, dimensions={0}, use_global_device_ids=true | all-gather | bytes 33280 | tf_op jit(solution)/shard_map/all_gather | solution.py:133
  302.8 3.6 multiply_reduce_fusion.2
  306.4 2.0 pad_maximum_fusion
  308.4 100.8 %psum.56 = f32[3,32]{1,0:T(4,128)S(1)} all-reduce(f32[3,32]{1,0:T(4,128)S(1)} %broadcast_select_fusion.15), channel_id=1, replica_groups=mesh['dp'=64,'mp'=8] {'dp','mp'}, use_global_device_ids=true, to_apply=%region_9.10 | all-reduce | flops 96 | bytes 768 | tf_op jit(solution)/shard_map/psum | solution.py:125
  412.7 1.7 multiply_add_fusion.1
  414.4 4.7 collective-permute-start.1
  419.3 48.0 %collective-permute-done.1 = f32[64,2048]{1,0:T(8,128)S(1)} collective-permute-done((f32[64,2048]{1,0:T(8,128)S(1)}, f32[64,2048]{1,0:T(8,128)S(1)}, u32[]{:S(2)}, u32[]{:S(2)}) %collective-permute-start.1) | collective-permute-done | bytes 524320 | tf_op jit(solution)/shard_map/ppermute | solution.py:16
  468.2 2.0 pad_maximum_fusion.1
  470.2 99.7 %psum.57 = f32[3,16]{1,0:T(4,128)S(1)} all-reduce(f32[3,16]{1,0:T(4,128)S(1)} %broadcast_select_fusion.14), channel_id=1, replica_groups=mesh['dp'=64,'mp'=8] {'dp','mp'}, use_global_device_ids=true, to_apply=%region_14.15 | all-reduce | flops 48 | bytes 384 | tf_op jit(solution)/shard_map/psum | solution.py:125
  573.4 2.2 collective-permute-start.2
  575.7 14.2 %collective-permute-done.2 = f32[32,2048]{1,0:T(8,128)S(1)} collective-permute-done((f32[32,2048]{1,0:T(8,128)S(1)}, f32[32,2048]{1,0:T(8,128)S(1)}, u32[]{:S(2)}, u32[]{:S(2)}) %collective-permute-start.2) | collective-permute-done | bytes 262176 | tf_op jit(solution)/shard_map/ppermute | solution.py:16
  590.6 2.0 pad_maximum_fusion.2
  592.6 99.6 %psum.58 = f32[3,8]{1,0:T(4,128)S(1)} all-reduce(f32[3,8]{1,0:T(4,128)S(1)} %broadcast_select_fusion.13), channel_id=1, replica_groups=mesh['dp'=64,'mp'=8] {'dp','mp'}, use_global_device_ids=true, to_apply=%region_19.20 | all-reduce | flops 24 | bytes 192 | tf_op jit(solution)/shard_map/psum | solution.py:125
  695.6 2.8 collective-permute-start.3
  698.7 4.1 collective-permute-done.3
  703.4 2.0 pad_maximum_fusion.3
  705.5 98.5 %psum.59 = f32[3,4]{1,0:T(4,128)S(1)} all-reduce(f32[3,4]{1,0:T(4,128)S(1)} %broadcast_select_fusion.12), channel_id=1, replica_groups=mesh['dp'=64,'mp'=8] {'dp','mp'}, use_global_device_ids=true, to_apply=%region_24.25 | all-reduce | flops 12 | bytes 96 | tf_op jit(solution)/shard_map/psum | solution.py:125
  807.4 3.5 collective-permute-start.4
  810.9 4.1 collective-permute-done.4
  815.7 2.0 pad_maximum_fusion.4
  817.8 99.3 %psum.60 = f32[3,2]{0,1:T(2,128)S(1)} all-reduce(f32[3,2]{0,1:T(2,128)S(1)} %broadcast_select_fusion.16), channel_id=1, replica_groups=mesh['dp'=64,'mp'=8] {'dp','mp'}, use_global_device_ids=true, to_apply=%region_29.30 | all-reduce | flops 6 | bytes 48 | tf_op jit(solution)/shard_map/psum | solution.py:125
  920.4 2.2 collective-permute-start.5
  926.9 2.0 pad_maximum_fusion.5
  928.9 99.1 %psum.61 = f32[3,1]{0,1:T(1,128)S(1)} all-reduce(f32[3,1]{0,1:T(1,128)S(1)} %pad_maximum_fusion.5), channel_id=1, replica_groups=mesh['dp'=64,'mp'=8] {'dp','mp'}, use_global_device_ids=true, to_apply=%region_34.35 | all-reduce | flops 3 | bytes 24 | tf_op jit(solution)/shard_map/psum | solution.py:125
  1036.8 128.3 %all-gather.5.cloned.1.call-done = bf16[64,4,2048]{2,1,0:T(4,128)(2,1)} async-done(((bf16[1,4,2048]{2,1,0:T(4,128)(2,1)}), bf16[64,4,2048]{2,1,0:T(4,128)(2,1)}) %all-gather.5.cloned.1.call-update) | async-done | bytes 1048592 | tf_op jit(solution)/shard_map/all_gather | solution.py:176
  1165.2 2.1 reshape.760
  (270 shorter events, 72.7 us)
Async XLA Ops:
  7.2 43.0 %copy-start = (bf16[256,2048]{1,0:T(8,128)(2,1)S(1)}, bf16[256,2048]{1,0:T(8,128)(2,1)}, u32[]{:S(2)}) copy-start(bf16[256,2048]{1,0:T(8,128)(2,1)} %param.22) | copy-start | bytes 3145732
  7.2 1158.0 %all-gather.5.cloned.1.call-start = ((), (), s32[]{:S(2)}) async-start(), calls=%async_computation | async-start | bytes 1064960 | tf_op jit(solution)/shard_map/all_gather | solution.py:176
  15.4 34.8 %copy-start.4 = (bf16[128,2048]{1,0:T(8,128)(2,1)S(1)}, bf16[128,2048]{1,0:T(8,128)(2,1)}, u32[]{:S(2)}) copy-start(bf16[128,2048]{1,0:T(8,128)(2,1)} %param.23) | copy-start | bytes 1572868
  15.4 35.4 %copy-start.17 = (f32[128]{0:T(128)S(1)}, f32[128]{0:T(128)}, u32[]{:S(2)}) copy-start(f32[128]{0:T(128)} %param.21) | copy-start | bytes 1540
  26.7 2.9 copy-start.11
  26.7 2.9 copy-start.13
  29.7 0.6 copy-start.12
  30.4 0.6 copy-start.14
  44.1 2.9 copy-start.11
  44.1 2.9 copy-start.13
  47.1 0.6 copy-start.12
  47.8 0.6 copy-start.14
  50.1 0.6 copy-start.18
  50.1 1.9 copy-start.1
  50.1 2.0 copy-start.2
  50.1 2.0 copy-start.5
  50.2 2.0 copy-start.6
  50.2 2.0 copy-start.10
  50.2 2.0 copy-start.15
  50.2 2.0 copy-start.16
  50.2 4.1 copy-start.3
  50.7 1.4 copy-start.8
  50.8 1.3 copy-start.7
  52.1 0.7 copy-start.9
  55.4 247.4 %collective-permute-start = (f32[128,2048]{1,0:T(8,128)}, f32[128,2048]{1,0:T(8,128)}, u32[]{:S(2)}, u32[]{:S(2)}) collective-permute-start(f32[128,2048]{1,0:T(8,128)} %slice_select_fusion.1), channel_id=1, source_target_pairs={{0,256},{8,264},{16,272},{24,280},{32,288},{40,296},{48,304},{56,3... | collective-permute-start | bytes 3145736 | tf_op jit(solution)/shard_map/ppermute | solution.py:16
  414.4 52.9 %collective-permute-start.1 = (f32[64,2048]{1,0:T(8,128)S(1)}, f32[64,2048]{1,0:T(8,128)S(1)}, u32[]{:S(2)}, u32[]{:S(2)}) collective-permute-start(f32[64,2048]{1,0:T(8,128)S(1)} %slice_select_fusion.3), channel_id=1, source_target_pairs={{0,128},{8,136},{16,144},{24,152},{32,160},{40,168},{48,176},{56,1... | collective-permute-start | bytes 1572872 | tf_op jit(solution)/shard_map/ppermute | solution.py:16
  573.4 16.4 %collective-permute-start.2 = (f32[32,2048]{1,0:T(8,128)S(1)}, f32[32,2048]{1,0:T(8,128)S(1)}, u32[]{:S(2)}, u32[]{:S(2)}) collective-permute-start(f32[32,2048]{1,0:T(8,128)S(1)} %slice_select_fusion.5), channel_id=1, source_target_pairs={{0,64},{8,72},{16,80},{24,88},{32,96},{40,104},{48,112},{56,120},{... | collective-permute-start | bytes 786440 | tf_op jit(solution)/shard_map/ppermute | solution.py:16
  695.6 7.1 collective-permute-start.3
  807.4 7.7 collective-permute-start.4
  920.4 5.8 collective-permute-start.5
Sparse Core Ops, SparseCore 0:
  1032.0 133.1 all-gather.4
where the time goes:
time: 1180 us; the launch traced here: 1170 us
  blocking collectives  753 us (64%)
  waiting for transfers between devices  199 us (17%)
  other arithmetic  97 us (8%)
  matrix products  36.4 us (3%)
  between operations  35.8 us (3%)
  starting transfers between devices  31.2 us (3%)
  local copies, waits for them, and re-layouts  21.6 us (2%)
    psum x6, blocking collectives, combine_weights(): lax.psum(jnp.where(chosen, partial_value[:, None], 0.0), ('dp', 'mp'))  597 us
    all_gather x1, waiting for transfers between devices, per_device(): lax.all_gather(own_piece.astype(jnp.bfloat16), 'dp', axis=0, tiled=True)  128 us
    all_gather x1, blocking collectives, combine_small(): lax.all_gather(rate_vec[None, :], 'dp', axis=0, tiled=True)  72.6 us
    all_gather x1, blocking collectives, combine_small(): lax.all_gather(gain_vec[None, :], 'dp', axis=0, tiled=True)  71.5 us
    ppermute x6, waiting for transfers between devices, from_partner(): return lax.ppermute(value, axis, pairs)  70.8 us
    another operation x18, other arithmetic, span_step(): jax.scipy.linalg.solve_triangular(system, right, lower=True, unit_diagona...  45.6 us
    ppermute x6, starting transfers between devices, from_partner(): return lax.ppermute(value, axis, pairs)  31.1 us
  transfers between devices with their start and end apart: 7, of which 6 were waited for; matrix products, arithmetic and copies ran while one was open for 7% of the time, Pallas kernels for 0%

commit v1 on v0

v1 whole, which is shorter than its diff:
```python
import functools

import jax
import jax.numpy as jnp
from jax import lax
from jax.experimental import pallas as pl
from jax.experimental.pallas import tpu as pltpu
from jax.sharding import PartitionSpec as P

EPS = 1e-06
F32 = jnp.float32
BF16 = jnp.bfloat16
HIGH = lax.Precision.HIGHEST
TOK = 128
HD = 128
HEADS = 2
REPS = 64
N_Z = 16
N_Y = 4
N_MP = 8
TILE = 64
LIMIT = 48 * 1024 * 1024
NN = (((1,), (0,)), ((), ()))
NT = (((1,), (1,)), ((), ()))

Z_GROUPS = [[z * N_Y + y for z in range(N_Z)] for y in range(N_Y)]
Y_GROUPS = [[z * N_Y + y for y in range(N_Y)] for z in range(N_Z)]


def matmul(a, b, dims=NN):
    return lax.dot_general(a, b, dims, precision=HIGH, preferred_element_type=F32)


def places(shape):
    return (
        lax.broadcasted_iota(jnp.int32, shape, 0),
        lax.broadcasted_iota(jnp.int32, shape, 1),
    )


def unit_rows(raw):
    value = raw.astype(F32)
    return value / jnp.sqrt(jnp.sum(value * value, axis=-1, keepdims=True) + EPS)


def invert_all(systems):
    row, col = places((TOK, TOK))
    eye = (row == col).astype(F32)
    close = (row >> 3) == (col >> 3)
    first = [jnp.where(close, low, 0.0) for low in systems]
    second = [matmul(a, a) for a in first]
    fourth = [matmul(a, a) for a in second]
    out = [eye - a for a in first]
    out = [a + matmul(a, b) for a, b in zip(out, second)]
    out = [a + matmul(a, b) for a, b in zip(out, fourth)]
    for shift in (3, 4, 5, 6):
        off = ((row >> (shift + 1)) == (col >> (shift + 1))) & ((row >> shift) != (col >> shift))
        parts = [matmul(jnp.where(off, low, 0.0), a) for low, a in zip(systems, out)]
        out = [a - matmul(a, b) for a, b in zip(out, parts)]
    return out


def forward_kernel(
    q_ref, k_ref, v_ref, dec_ref, beta_ref, rate_ref, bias_ref, gain_ref, up_ref,
    g_ref, m_ref, l_ref, s_ref, a_ref, w_ref, o_ref,
):
    row, col = places((TOK, TOK))
    lower = row >= col
    strict = row > col
    query = unit_rows(q_ref[...]) * HD ** (-0.5)
    keys = unit_rows(k_ref[...])
    inner = matmul(keys, keys, NT)
    scores = matmul(query, keys, NT)
    pre = dec_ref[...] + bias_ref[...]
    soft = jnp.maximum(pre, 0.0) + jnp.log1p(jnp.exp(-jnp.abs(pre)))
    log_decay = -jnp.exp(rate_ref[...]) * soft
    beta = 1.0 / (1.0 + jnp.exp(-beta_ref[...]))
    cumul = matmul(lower.astype(F32), log_decay)
    mixers, systems = [], []
    for h in range(HEADS):
        wide = jnp.broadcast_to(cumul[:, h : h + 1], (TOK, TOK))
        spread = jnp.where(lower, wide - wide.T, 0.0)
        decay = jnp.where(lower, jnp.exp(spread), 0.0)
        mixers.append(scores * decay)
        systems.append(jnp.where(strict, beta[:, h : h + 1] * inner * decay, 0.0))
        m_ref[h] = mixers[h]
        l_ref[h] = systems[h]
        s_ref[h] = spread
    inverses = invert_all(systems)
    writes = [
        matmul(inverses[h], beta[:, h : h + 1] * v_ref[:, h * HD : (h + 1) * HD].astype(F32))
        for h in range(HEADS)
    ]
    mixed = [matmul(mixers[h], writes[h]) for h in range(HEADS)]
    normed = []
    for h in range(HEADS):
        a_ref[h] = inverses[h]
        w_ref[h] = writes[h]
        o_ref[h] = mixed[h]
        scale = lax.rsqrt(jnp.mean(mixed[h] * mixed[h], axis=-1, keepdims=True) + EPS)
        normed.append((mixed[h] * scale * gain_ref[...]).T.astype(BF16))
    left = jnp.concatenate(normed, axis=0)
    for z in range(N_Z):
        part = lax.dot_general(
            left, up_ref[:, z * HD : (z + 1) * HD], NN, preferred_element_type=F32
        ).astype(BF16)
        for y in range(N_Y):
            g_ref[z * N_Y + y] = part[y * TILE : (y + 1) * TILE, :]


def backward_kernel(
    place_ref, m_ref, l_ref, s_ref, a_ref, w_ref, o_ref, gain_ref, weight_ref, up_ref, out_ref
):
    gain = gain_ref[...]
    d_normed = lax.dot_general(up_ref[...], weight_ref[...], NT, preferred_element_type=F32)
    lane = lax.broadcasted_iota(jnp.int32, (1, HD), 1)
    heads = range(HEADS)
    turns = [matmul(l_ref[h] * s_ref[h], w_ref[h]) for h in heads]
    turns = [matmul(a_ref[h], turns[h]) for h in heads]
    slopes = [matmul(m_ref[h] * s_ref[h], w_ref[h]) - matmul(m_ref[h], turns[h]) for h in heads]
    grad_gain = jnp.zeros((1, HD), F32)
    rates = jnp.zeros((1, HD), F32)
    for h in heads:
        mixed = o_ref[h]
        scale = lax.rsqrt(jnp.mean(mixed * mixed, axis=-1, keepdims=True) + EPS)
        unit = mixed * scale
        given = d_normed[:, h * HD : (h + 1) * HD]
        grad_gain = grad_gain + jnp.sum(unit * given, axis=0, keepdims=True)
        tilted = given * gain
        d_mixed = scale * (tilted - unit * jnp.mean(unit * tilted, axis=-1, keepdims=True))
        rate = jnp.sum(jnp.sum(d_mixed * slopes[h], axis=0, keepdims=True), axis=1, keepdims=True)
        rates = rates + jnp.where(lane == place_ref[0] * HEADS + h, rate, 0.0)
    out_ref[...] = jnp.concatenate([grad_gain, rates], axis=0)


def gram_kernel(x_ref, small_ref, out_ref, wide):
    wide[...] = x_ref[...].astype(F32).reshape(REPS * TILE, HD)
    total = jnp.zeros((REPS, REPS), F32)
    for f in range(0, TILE, 2):
        rows = jnp.concatenate(
            [wide[pl.ds(f + e, REPS, stride=TILE), :].astype(BF16) for e in range(2)], axis=1
        )
        total = total + lax.dot_general(rows, rows, NT, preferred_element_type=F32)
    half = jnp.concatenate([total[: REPS // 2], total[REPS // 2 :]], axis=1)
    small = small_ref[...]
    fill = jnp.zeros((2, HD), F32)
    for m in range(N_MP):
        out_ref[m] = jnp.concatenate([half[4 * m : 4 * m + 4], small, fill], axis=0)


def spread_kernel(in_ref, out_ref):
    total = in_ref[0]
    for m in range(1, N_MP):
        total = total + in_ref[m]
    out_ref[...] = jnp.broadcast_to(total[None], out_ref.shape)


def small_tree(stack):
    half = REPS // 2
    while half:
        other = pltpu.roll(stack, half, 0)
        inner = jnp.sum(stack * other, axis=1, keepdims=True)
        norm = jnp.sum(stack * stack, axis=1, keepdims=True)
        part = (1.0 - inner / (2.0 * (norm + EPS))) * stack
        stack = part + pltpu.roll(part, half, 0)
        half //= 2
    return stack[0:1]


def gather_kernel(in_ref, gram_ref, gain_ref, rate_ref):
    total = in_ref[0, 0:4]
    for r in range(1, REPS):
        total = total + in_ref[r, 0:4]
    gram_ref[...] = jnp.broadcast_to(total[None], gram_ref.shape)
    flat = in_ref[...].reshape(REPS * 8, HD)
    gains = jnp.concatenate([flat[8 * r + 4 : 8 * r + 5] for r in range(REPS)], axis=0)
    rates = jnp.concatenate([flat[8 * r + 5 : 8 * r + 6] for r in range(REPS)], axis=0)
    gain_ref[...] = small_tree(gains)
    rate_ref[...] = small_tree(rates)


def path_coefs(gram):
    row, lane = places((REPS, HD))
    same = row == (lane & (REPS - 1))
    near = row == lane
    coefs = jnp.ones((REPS, 1), F32)
    half = REPS // 2
    while half:
        other = pltpu.roll(gram, half, 1)
        norm_col = jnp.sum(jnp.where(near, gram, 0.0), axis=1, keepdims=True)
        inner_col = jnp.sum(jnp.where(near, other, 0.0), axis=1, keepdims=True)
        norm_row = jnp.sum(jnp.where(same, gram, 0.0), axis=0, keepdims=True)
        inner_row = jnp.sum(jnp.where(same, other, 0.0), axis=0, keepdims=True)
        by_col = 1.0 - inner_col / (2.0 * (norm_col + EPS))
        by_row = 1.0 - inner_row / (2.0 * (norm_row + EPS))
        coefs = coefs * by_col
        part = by_col * by_row * gram
        part = part + pltpu.roll(part, half, 1)
        gram = part + pltpu.roll(part, half, 0)
        half //= 2
    return coefs


def combine_kernel(gram_ref, x_ref, out_ref, factor):
    lane = lax.broadcasted_iota(jnp.int32, (REPS // 2, HD), 1)
    packed = gram_ref[...].reshape(REPS // 2, HD)
    turned = pltpu.roll(packed, REPS, 1)
    gram = jnp.concatenate(
        [jnp.where(lane < REPS, packed, turned), jnp.where(lane < REPS, turned, packed)], axis=0
    )
    factor[...] = jnp.broadcast_to(path_coefs(gram), (REPS, HD))
    total = jnp.zeros((TILE, HD), F32)
    for r in range(REPS):
        total = total + factor[r : r + 1, :] * x_ref[r].astype(F32)
    out_ref[...] = jnp.broadcast_to(total.astype(BF16)[None], out_ref.shape)


def call(body, outs, ops, scratch=(), smem=(), flops=0):
    size = sum(o.size * o.dtype.itemsize for o in ops) + sum(o.size * o.dtype.itemsize for o in outs)
    specs = [
        pl.BlockSpec(memory_space=pltpu.SMEM if i in smem else pltpu.VMEM) for i in range(len(ops))
    ]
    return pl.pallas_call(
        body,
        out_shape=outs,
        in_specs=specs,
        out_specs=[pl.BlockSpec(memory_space=pltpu.VMEM) for _ in outs],
        scratch_shapes=list(scratch),
        compiler_params=pltpu.CompilerParams(vmem_limit_bytes=LIMIT),
        cost_estimate=pl.CostEstimate(flops=flops, bytes_accessed=size, transcendentals=0),
    )(*ops)


def shape(dims, dtype=F32):
    return jax.ShapeDtypeStruct(dims, dtype)


def per_device(
    query_raw, key_raw, values, decay_input, beta_input, log_rate, step_bias, gain, out_weight, upstream
):
    gain_row = gain[None, :]
    square = shape((HEADS, TOK, TOK))
    tiles, *saved = call(
        forward_kernel,
        [shape((REPS, TILE, HD), BF16)] + [square] * 6,
        [
            query_raw, key_raw, values, decay_input, beta_input,
            log_rate[None, :], step_bias[None, :], gain_row, upstream,
        ],
        flops=2 * 10**9,
    )
    stack = lax.all_to_all(tiles, "dp", 0, 0)
    place = lax.axis_index("mp").astype(jnp.int32)[None]
    (small,) = call(
        backward_kernel,
        [shape((2, HD))],
        [place, *saved, gain_row, out_weight, upstream],
        smem=(0,),
        flops=2 * 10**9,
    )
    (gram_part,) = call(
        gram_kernel,
        [shape((N_MP, 8, HD))],
        [stack, small],
        scratch=[pltpu.VMEM((REPS * TILE, HD), F32)],
        flops=10**9,
    )
    gram_part = lax.all_to_all(gram_part, "mp", 0, 0)
    (gram_part,) = call(spread_kernel, [shape((REPS, 8, HD))], [gram_part])
    gram_part = lax.all_to_all(gram_part, "dp", 0, 0)
    gram_part, gain_final, rate_final = call(
        gather_kernel, [shape((N_MP, 4, HD)), shape((1, HD)), shape((1, HD))], [gram_part]
    )
    gram = lax.all_to_all(gram_part, "mp", 0, 0)
    (whole,) = call(
        combine_kernel,
        [shape((N_Z, TILE, HD), BF16)],
        [gram, stack],
        scratch=[pltpu.VMEM((REPS, HD), F32)],
        flops=10**8,
    )
    whole = lax.all_to_all(whole, "dp", 0, 0, axis_index_groups=Z_GROUPS)
    whole = jnp.broadcast_to(whole[None], (N_Y,) + whole.shape)
    whole = lax.all_to_all(whole, "dp", 0, 0, axis_index_groups=Y_GROUPS)
    whole = jnp.transpose(whole, (0, 2, 1, 3)).reshape(N_Y * TILE, N_Z * HD)
    return (whole, gain_final[0], rate_final[0, : HEADS * N_MP])


def solution(mesh):
    in_specs = (
        P("dp", "mp"),
        P("dp", "mp"),
        P("dp", "mp"),
        P("dp", "mp"),
        P("dp", "mp"),
        P("mp"),
        P("mp"),
        P(),
        P("mp", None),
        P("dp", None),
    )
    out_specs = (P("mp", None), P(), P())
    return jax.shard_map(
        per_device, mesh=mesh, in_specs=in_specs, out_specs=out_specs, check_vma=False
    )
```

time: 1180 us -> 175 us (0.15)
  the two profiles are of different devices: /device:TPU:2 before, /device:TPU:32 now
where the time goes in v1:
time: 175 us; the launch traced here: 174 us
  blocking collectives  67.5 us (39%)
  waiting for transfers between devices  66 us (38%)
  starting transfers between devices  22.9 us (13%)
  Pallas kernels  11.2 us (6%)
  local copies, waits for them, and re-layouts  5.69 us (3%)
    all_to_all x1, waiting for transfers between devices, per_device(): stack = lax.all_to_all(tiles, 'dp', 0, 0)  52.7 us
    all_to_all x1, blocking collectives, per_device(): gram_part = lax.all_to_all(gram_part, 'dp', 0, 0)  28.7 us
    all_to_all x1, blocking collectives, per_device(): whole = lax.all_to_all(whole, 'dp', 0, 0, axis_index_groups=Z_GROUPS)  21.6 us
    all_to_all x1, starting transfers between devices, per_device(): stack = lax.all_to_all(tiles, 'dp', 0, 0)  18.5 us
    all_to_all x1, waiting for transfers between devices, per_device(): whole = lax.all_to_all(whole, 'dp', 0, 0, axis_index_groups=Y_GROUPS)  13.3 us
    pallas_call x6, Pallas kernels, call(): pl.pallas_call(body, out_shape=outs, in_specs=specs, out_specs=[pl.BlockS...  11.2 us
    all_to_all x1, blocking collectives, per_device(): gram_part = lax.all_to_all(gram_part, 'mp', 0, 0)  9.55 us
    all_to_all x1, blocking collectives, per_device(): gram = lax.all_to_all(gram_part, 'mp', 0, 0)  7.71 us
  transfers between devices with their start and end apart: 2, of which 2 were waited for; matrix products, arithmetic and copies ran while one was open for 0% of the time, Pallas kernels for 1%

profile of v1, /device:TPU:32, one launch (start us, length us, event | category | flops | bytes accessed | tf_op | source)
XLA Modules:
  0.0 174.1 jit_solution(12304812617256521037)
XLA Ops:
  0.6 0.0 copy-start.9
  0.6 0.0 copy-start.3
  0.7 0.8 copy.13.dec_ref
  1.5 0.0 copy-done.9
  1.5 0.0 copy-start.4
  1.5 0.0 copy-start.5
  1.5 0.1 copy.14.beta_ref
  1.6 0.0 copy-start.6
  1.6 0.0 copy-start.7
  1.6 0.0 copy-start.8
  1.6 0.0 copy-done.3
  1.7 0.6 copy-done.4
  2.2 0.0 copy-done.5
  2.3 0.0 copy-done.6
  2.3 0.0 copy-done.7
  2.3 0.0 copy-done.8
  2.3 0.0 copy-start.1
  2.3 1.0 copy-done.1
  3.3 5.4 %shard_map.121 = (bf16[64,64,128]{2,1,0:T(8,128)(2,1)}, f32[2,128,128]{2,1,0:T(8,128)S(1)}, f32[2,128,128]{2,1,0:T(8,128)S(1)}, f32[2,128,128]{2,1,0:T(8,128)S(1...) custom-call(bf16[128,128]{1,0:T(8,128)(2,1)S(1)} %copy-done.4, ...), custom_call_target="tpu_custom_call" | custom-call | flops 2000000000 | bytes 2492944 | tf_op jit(solution)/shard_map/pallas_call | solution.py:223
  8.7 0.0 copy-start
  8.7 0.0 copy-start.2
  8.7 18.5 %all-to-all-start = ((bf16[64,64,128]{2,1,0:T(8,128)(2,1)}), bf16[64,64,128]{2,1,0:T(8,128)(2,1)S(1)}, u32[]{:S(2)}, u32[]{:S(2)}) async-start(bf16[64,64,128]{2,1,0:T(8,128)(2,1)} %get-tuple-element.13), calls=%async_computation | async-start | bytes 2097152 | tf_op jit(solution)/shard_map/all_to_all | solution.py:252
  27.2 0.0 copy-done
  27.3 0.0 copy-done.2
  27.3 1.4 shard_map.122.small_ref
  28.7 52.7 %all-to-all-done.x_ref = bf16[64,64,128]{2,1,0:T(8,128)(2,1)S(1)} async-done(((bf16[64,64,128]{2,1,0:T(8,128)(2,1)}), bf16[64,64,128]{2,1,0:T(8,128)(2,1)S(1)}, u32[]{:S(2)}, u32[]{:S(2)}) %all-to-all-start) | async-done | bytes 1048608 | tf_op jit(solution)/shard_map/all_to_all | solution.py:252
  81.4 1.7 shard_map.123
  83.1 9.5 %all_to_all.30.in_ref = f32[8,8,128]{2,1,0:T(8,128)S(1)} all-to-all(f32[8,8,128]{2,1,0:T(8,128)S(1)} %shard_map.123), channel_id=1, replica_groups=mesh['dp'=64,'mp'=8] {'mp'}, dimensions={0} | all-to-all | bytes 65536 | tf_op jit(solution)/shard_map/all_to_all | solution.py:268
  92.7 28.7 %all_to_all.31.in_ref = f32[64,8,128]{2,1,0:T(8,128)S(1)} all-to-all(f32[64,8,128]{2,1,0:T(8,128)S(1)} %shard_map.124), channel_id=1, replica_groups=mesh['dp'=64,'mp'=8] {'dp'}, dimensions={0} | all-to-all | bytes 524288 | tf_op jit(solution)/shard_map/all_to_all | solution.py:270
  121.3 1.1 shard_map.125
  122.4 7.7 %all_to_all.32.gram_ref = f32[8,4,128]{2,1,0:T(4,128)S(1)} all-to-all(f32[8,4,128]{2,1,0:T(4,128)S(1)} %get-tuple-element.20), channel_id=1, replica_groups=mesh['dp'=64,'mp'=8] {'mp'}, dimensions={0} | all-to-all | bytes 32768 | tf_op jit(solution)/shard_map/all_to_all | solution.py:274
  130.1 1.6 shard_map.126
  131.7 21.6 %all_to_all.33 = bf16[16,64,128]{2,1,0:T(8,128)(2,1)S(1)} all-to-all(bf16[16,64,128]{2,1,0:T(8,128)(2,1)S(1)} %shard_map.126), channel_id=1, replica_groups={{0,32,64,96,128,160,192,224,256,288,320,352,384,416,448,480},{8,40,72,1..., dimensions={0} | all-to-all | bytes 524288 | tf_op jit(solution)/shard_map/all_to_all | solution.py:282
  153.3 0.2 copy.15
  153.5 1.1 broadcast_in_dim.22
  154.6 4.4 %all-to-all-start.5 = ((bf16[4,16,64,128]{3,1,2,0:T(8,128)(2,1)}), bf16[4,16,64,128]{3,1,2,0:T(8,128)(2,1)S(1)}, u32[]{:S(2)}, u32[]{:S(2)}) async-start(bf16[4,16,64,128]{3,1,2,0:T(8,128)(2,1)} %broadcast_in_dim.22), calls=%async_computation.5 | async-start | bytes 2097152 | tf_op jit(solution)/shard_map/all_to_all | solution.py:284
  159.0 0.5 slice_bitcast_fusion
  159.5 13.3 %all-to-all-done.5 = bf16[4,16,64,128]{3,1,2,0:T(8,128)(2,1)S(1)} async-done(((bf16[4,16,64,128]{3,1,2,0:T(8,128)(2,1)}), bf16[4,16,64,128]{3,1,2,0:T(8,128)(2,1)S(1)}, u32[]{:S(2)}, u32[]{:S(2)}) %all-to-all-start.5) | async-done | bytes 1048608 | tf_op jit(solution)/shard_map/all_to_all | solution.py:284
  172.8 1.2 copy.18
  (1 shorter events, 0.0 us)
Async XLA Ops:
  0.6 0.8 copy-start.9
  0.6 1.0 copy-start.3
  1.5 0.8 copy-start.4
  1.5 0.8 copy-start.5
  1.6 0.7 copy-start.6
  1.6 0.7 copy-start.7
  1.6 0.7 copy-start.8
  2.3 1.0 copy-start.1
  8.7 18.5 %copy-start = (bf16[256,2048]{1,0:T(8,128)(2,1)S(1)}, bf16[256,2048]{1,0:T(8,128)(2,1)}, u32[]{:S(2)}) copy-start(bf16[256,2048]{1,0:T(8,128)(2,1)} %weight_ref.1) | copy-start | bytes 3145732
  8.7 18.5 %copy-start.2 = (bf16[128,2048]{1,0:T(8,128)(2,1)S(1)}, bf16[128,2048]{1,0:T(8,128)(2,1)}, u32[]{:S(2)}) copy-start(bf16[128,2048]{1,0:T(8,128)(2,1)} %up_ref.3) | copy-start | bytes 1572868
  8.7 72.7 %all-to-all-start = ((bf16[64,64,128]{2,1,0:T(8,128)(2,1)}), bf16[64,64,128]{2,1,0:T(8,128)(2,1)S(1)}, u32[]{:S(2)}, u32[]{:S(2)}) async-start(bf16[64,64,128]{2,1,0:T(8,128)(2,1)} %get-tuple-element.13), calls=%async_computation | async-start | bytes 2097152 | tf_op jit(solution)/shard_map/all_to_all | solution.py:252
  154.6 18.2 %all-to-all-start.5 = ((bf16[4,16,64,128]{3,1,2,0:T(8,128)(2,1)}), bf16[4,16,64,128]{3,1,2,0:T(8,128)(2,1)S(1)}, u32[]{:S(2)}, u32[]{:S(2)}) async-start(bf16[4,16,64,128]{3,1,2,0:T(8,128)(2,1)} %broadcast_in_dim.22), calls=%async_computation.5 | async-start | bytes 2097152 | tf_op jit(solution)/shard_map/all_to_all | solution.py:284

commit v2 on v1

v2 whole, which is shorter than its diff:
```python
import functools

import jax
import jax.numpy as jnp
from jax import lax
from jax.experimental import pallas as pl
from jax.experimental.pallas import tpu as pltpu
from jax.sharding import PartitionSpec as P

EPS = 1e-06
F32 = jnp.float32
BF16 = jnp.bfloat16
HIGH = lax.Precision.HIGHEST
TOK = 128
HD = 128
HEADS = 2
REPS = 64
N_Z = 16
N_Y = 4
N_MP = 8
TILE = 64
LIMIT = 48 * 1024 * 1024
NN = (((1,), (0,)), ((), ()))
NT = (((1,), (1,)), ((), ()))

Z_GROUPS = [[z * N_Y + y for z in range(N_Z)] for y in range(N_Y)]
Y_GROUPS = [[z * N_Y + y for y in range(N_Y)] for z in range(N_Z)]
PLANES = [[z * N_Y * N_MP + i for i in range(N_Y * N_MP)] for z in range(N_Z)]


def matmul(a, b, dims=NN):
    return lax.dot_general(a, b, dims, precision=HIGH, preferred_element_type=F32)


def places(shape):
    return (
        lax.broadcasted_iota(jnp.int32, shape, 0),
        lax.broadcasted_iota(jnp.int32, shape, 1),
    )


def unit_rows(raw):
    value = raw.astype(F32)
    return value / jnp.sqrt(jnp.sum(value * value, axis=-1, keepdims=True) + EPS)


def invert_all(systems):
    row, col = places((TOK, TOK))
    eye = (row == col).astype(F32)
    close = (row >> 3) == (col >> 3)
    first = [jnp.where(close, low, 0.0) for low in systems]
    second = [matmul(a, a) for a in first]
    fourth = [matmul(a, a) for a in second]
    out = [eye - a for a in first]
    out = [a + matmul(a, b) for a, b in zip(out, second)]
    out = [a + matmul(a, b) for a, b in zip(out, fourth)]
    for shift in (3, 4, 5, 6):
        off = ((row >> (shift + 1)) == (col >> (shift + 1))) & ((row >> shift) != (col >> shift))
        parts = [matmul(jnp.where(off, low, 0.0), a) for low, a in zip(systems, out)]
        out = [a - matmul(a, b) for a, b in zip(out, parts)]
    return out


def small_inputs(dec_ref, beta_ref, rate_ref, bias_ref):
    row, col = places((TOK, TOK))
    falls = []
    for h in range(HEADS):
        pre = dec_ref[h : h + 1, :] + bias_ref[:, h : h + 1]
        soft = jnp.maximum(pre, 0.0) + jnp.log1p(jnp.exp(-jnp.abs(pre)))
        falls.append(-jnp.exp(rate_ref[:, h : h + 1]) * soft)
    cumul = matmul(jnp.concatenate(falls, axis=0), (row <= col).astype(F32))
    return cumul, 1.0 / (1.0 + jnp.exp(-beta_ref[...]))


def delta_parts(cumul, beta, inner, scores):
    row, col = places((TOK, TOK))
    lower = row >= col
    strict = row > col
    mixers, systems, spreads, strengths = [], [], [], []
    for h in range(HEADS):
        wide = jnp.broadcast_to(cumul[h : h + 1, :], (TOK, TOK))
        spread = jnp.where(lower, wide.T - wide, 0.0)
        decay = jnp.where(lower, jnp.exp(spread), 0.0)
        strength = jnp.broadcast_to(beta[h : h + 1, :], (TOK, TOK)).T
        mixers.append(scores * decay)
        systems.append(jnp.where(strict, strength * inner * decay, 0.0))
        spreads.append(spread)
        strengths.append(strength)
    return mixers, systems, spreads, strengths


def forward_kernel(
    k_any, q_any, v_any, up_any, dec_ref, beta_ref, rate_ref, bias_ref, gain_ref,
    g_any, k_ref, q_ref, v_ref, up_ref, g_ref, in_sems, out_sems,
):
    pairs = ((k_any, k_ref), (q_any, q_ref), (v_any, v_ref), (up_any, up_ref))
    fetches = [pltpu.make_async_copy(a, b, in_sems.at[i]) for i, (a, b) in enumerate(pairs)]
    for fetch in fetches:
        fetch.start()
    cumul, beta = small_inputs(dec_ref, beta_ref, rate_ref, bias_ref)
    heads = range(HEADS)
    fetches[0].wait()
    keys = unit_rows(k_ref[...])
    inner = matmul(keys, keys, NT)
    fetches[1].wait()
    scores = matmul(unit_rows(q_ref[...]) * HD ** (-0.5), keys, NT)
    mixers, systems, _, strengths = delta_parts(cumul, beta, inner, scores)
    inverses = invert_all(systems)
    fetches[2].wait()
    scaled = [strengths[h] * v_ref[:, h * HD : (h + 1) * HD].astype(F32) for h in heads]
    writes = [matmul(inverses[h], scaled[h]) for h in heads]
    mixed = [matmul(mixers[h], writes[h]) for h in heads]
    normed = []
    for h in heads:
        scale = lax.rsqrt(jnp.mean(mixed[h] * mixed[h], axis=-1, keepdims=True) + EPS)
        normed.append((mixed[h] * scale * gain_ref[...]).T.astype(BF16))
    left = jnp.concatenate(normed, axis=0)
    fetches[3].wait()
    stores = []
    for z in range(N_Z):
        part = lax.dot_general(
            left, up_ref[:, z * HD : (z + 1) * HD], NN, preferred_element_type=F32
        ).astype(BF16)
        for y in range(N_Y):
            g_ref[z * N_Y + y] = part[y * TILE : (y + 1) * TILE, :]
        tiles = pl.ds(z * N_Y, N_Y)
        stores.append(pltpu.make_async_copy(g_ref.at[tiles], g_any.at[tiles], out_sems.at[z]))
        stores[z].start()
    for store in stores:
        store.wait()


def backward_kernel(
    place_ref, k_any, q_any, v_any, up_any, weight_any, _, dec_ref, beta_ref, rate_ref, bias_ref,
    gain_ref, out_ref, k_ref, q_ref, v_ref, up_ref, weight_ref, in_sems,
):
    pairs = (
        (k_any, k_ref), (q_any, q_ref), (v_any, v_ref), (up_any, up_ref), (weight_any, weight_ref)
    )
    fetches = [pltpu.make_async_copy(a, b, in_sems.at[i]) for i, (a, b) in enumerate(pairs)]
    for fetch in fetches:
        fetch.start()
    for fetch in fetches:
        fetch.wait()
    gain = gain_ref[...]
    d_normed = lax.dot_general(up_ref[...], weight_ref[...], NT, preferred_element_type=F32)
    lane = lax.broadcasted_iota(jnp.int32, (1, HD), 1)
    heads = range(HEADS)
    keys = unit_rows(k_ref[...])
    inner = matmul(keys, keys, NT)
    scores = matmul(unit_rows(q_ref[...]) * HD ** (-0.5), keys, NT)
    cumul, beta = small_inputs(dec_ref, beta_ref, rate_ref, bias_ref)
    mixers, systems, spreads, strengths = delta_parts(cumul, beta, inner, scores)
    inverses = invert_all(systems)
    scaled = [strengths[h] * v_ref[:, h * HD : (h + 1) * HD].astype(F32) for h in heads]
    writes = [matmul(inverses[h], scaled[h]) for h in heads]
    outs = [matmul(mixers[h], writes[h]) for h in heads]
    turns = [matmul(systems[h] * spreads[h], writes[h]) for h in heads]
    turns = [matmul(inverses[h], turns[h]) for h in heads]
    slopes = [
        matmul(mixers[h] * spreads[h], writes[h]) - matmul(mixers[h], turns[h]) for h in heads
    ]
    grad_gain = jnp.zeros((1, HD), F32)
    rates = jnp.zeros((1, HD), F32)
    for h in heads:
        mixed = outs[h]
        scale = lax.rsqrt(jnp.mean(mixed * mixed, axis=-1, keepdims=True) + EPS)
        unit = mixed * scale
        given = d_normed[:, h * HD : (h + 1) * HD]
        grad_gain = grad_gain + jnp.sum(unit * given, axis=0, keepdims=True)
        tilted = given * gain
        d_mixed = scale * (tilted - unit * jnp.mean(unit * tilted, axis=-1, keepdims=True))
        rate = jnp.sum(jnp.sum(d_mixed * slopes[h], axis=0, keepdims=True), axis=1, keepdims=True)
        rates = rates + jnp.where(lane == place_ref[0] * HEADS + h, rate, 0.0)
    out_ref[...] = jnp.concatenate([grad_gain, rates], axis=0)


def gram_kernel(place_ref, x_ref, small_ref, out_ref, wide):
    wide[...] = x_ref[...].astype(F32).reshape(REPS * TILE, HD)
    total = jnp.zeros((REPS, REPS), F32)
    for f in range(0, TILE, 2):
        rows = jnp.concatenate(
            [wide[pl.ds(f + e, REPS, stride=TILE), :].astype(BF16) for e in range(2)], axis=1
        )
        total = total + lax.dot_general(rows, rows, NT, preferred_element_type=F32)
    half = jnp.concatenate([total[: REPS // 2], total[REPS // 2 :]], axis=1)
    fill = jnp.zeros((3, HD), F32)
    for m in range(N_MP):
        kind, y = divmod(m, N_Y)
        extra = jnp.where(place_ref[0] == y, small_ref[kind : kind + 1, :], 0.0)
        block = jnp.concatenate([half[4 * m : 4 * m + 4], extra, fill], axis=0)
        for target in range(N_Y):
            out_ref[target * N_MP + m] = block


def spread_kernel(in_ref, out_ref):
    total = in_ref[0]
    for m in range(1, N_Y * N_MP):
        total = total + in_ref[m]
    out_ref[...] = jnp.broadcast_to(total[None], out_ref.shape)


def gather_kernel(in_ref, out_ref):
    total = in_ref[0, 0:4]
    for z in range(1, N_Z):
        total = total + in_ref[z, 0:4]
    fill = jnp.zeros((4, HD), F32)
    block = jnp.concatenate([total, fill] + [in_ref[z, 4:5] for z in range(N_Z)], axis=0)
    out_ref[...] = jnp.broadcast_to(block[None], out_ref.shape)


def small_tree(stack):
    half = REPS // 2
    while half:
        other = pltpu.roll(stack, half, 0)
        inner = jnp.sum(stack * other, axis=1, keepdims=True)
        norm = jnp.sum(stack * stack, axis=1, keepdims=True)
        part = (1.0 - inner / (2.0 * (norm + EPS))) * stack
        stack = part + pltpu.roll(part, half, 0)
        half //= 2
    return stack[0:1]


def trees_kernel(in_ref, gain_ref, rate_ref):
    for kind, out in enumerate((gain_ref, rate_ref)):
        rows = [in_ref[kind * N_Y + r % N_Y, 8 + r // N_Y : 9 + r // N_Y, :] for r in range(REPS)]
        out[...] = small_tree(jnp.concatenate(rows, axis=0))


def path_coefs(gram):
    row, lane = places((REPS, HD))
    same = row == (lane & (REPS - 1))
    near = row == lane
    coefs = jnp.ones((REPS, 1), F32)
    half = REPS // 2
    while half:
        other = pltpu.roll(gram, half, 1)
        norm_col = jnp.sum(jnp.where(near, gram, 0.0), axis=1, keepdims=True)
        inner_col = jnp.sum(jnp.where(near, other, 0.0), axis=1, keepdims=True)
        norm_row = jnp.sum(jnp.where(same, gram, 0.0), axis=0, keepdims=True)
        inner_row = jnp.sum(jnp.where(same, other, 0.0), axis=0, keepdims=True)
        by_col = 1.0 - inner_col / (2.0 * (norm_col + EPS))
        by_row = 1.0 - inner_row / (2.0 * (norm_row + EPS))
        coefs = coefs * by_col
        part = by_col * by_row * gram
        part = part + pltpu.roll(part, half, 1)
        gram = part + pltpu.roll(part, half, 0)
        half //= 2
    return coefs


def combine_kernel(gram_ref, x_ref, out_ref, factor):
    lane = lax.broadcasted_iota(jnp.int32, (REPS // 2, HD), 1)
    packed = jnp.concatenate([gram_ref[m, 0:4] for m in range(N_MP)], axis=0)
    turned = pltpu.roll(packed, REPS, 1)
    gram = jnp.concatenate(
        [jnp.where(lane < REPS, packed, turned), jnp.where(lane < REPS, turned, packed)], axis=0
    )
    factor[...] = jnp.broadcast_to(path_coefs(gram), (REPS, HD))
    total = jnp.zeros((TILE, HD), F32)
    for r in range(REPS):
        total = total + factor[r : r + 1, :] * x_ref[r].astype(F32)
    out_ref[...] = jnp.broadcast_to(total.astype(BF16)[None], out_ref.shape)


def unfold_kernel(in_ref, out_ref):
    for z in range(N_Z):
        out_ref[:, :, z * HD : (z + 1) * HD] = jnp.broadcast_to(
            in_ref[z][None], (N_Y, TILE, HD)
        )


def call(body, outs, ops, scratch=(), smem=(), hbm=(), out_hbm=(), flops=0, limit=LIMIT):
    size = sum(o.size * o.dtype.itemsize for o in ops) + sum(o.size * o.dtype.itemsize for o in outs)
    spaces = [
        pltpu.SMEM if i in smem else pl.ANY if i in hbm else pltpu.VMEM for i in range(len(ops))
    ]
    return pl.pallas_call(
        body,
        out_shape=outs,
        in_specs=[pl.BlockSpec(memory_space=space) for space in spaces],
        out_specs=[
            pl.BlockSpec(memory_space=pl.ANY if i in out_hbm else pltpu.VMEM)
            for i in range(len(outs))
        ],
        scratch_shapes=list(scratch),
        compiler_params=pltpu.CompilerParams(vmem_limit_bytes=limit),
        cost_estimate=pl.CostEstimate(flops=flops, bytes_accessed=size, transcendentals=0),
    )(*ops)


def shape(dims, dtype=F32):
    return jax.ShapeDtypeStruct(dims, dtype)


def forward(big, rows, gain_row):
    (tiles,) = call(
        forward_kernel,
        [shape((REPS, TILE, HD), BF16)],
        [*big, *rows, gain_row],
        scratch=[pltpu.VMEM(a.shape, BF16) for a in big]
        + [
            pltpu.VMEM((REPS, TILE, HD), BF16),
            pltpu.SemaphoreType.DMA((4,)),
            pltpu.SemaphoreType.DMA((N_Z,)),
        ],
        hbm=(0, 1, 2, 3),
        out_hbm=(0,),
        limit=56 * 2**20,
        flops=2 * 10**9,
    )
    return tiles


def backward(place, big, tiles, rows, gain_row):
    (small,) = call(
        backward_kernel,
        [shape((2, HD))],
        [place, *big, tiles, *rows, gain_row],
        scratch=[pltpu.VMEM(a.shape, BF16) for a in big] + [pltpu.SemaphoreType.DMA((5,))],
        smem=(0,),
        hbm=(1, 2, 3, 4, 5, 6),
        limit=56 * 2**20,
        flops=2 * 10**9,
    )
    return small


def gram(stack, small, place):
    (part,) = call(
        gram_kernel,
        [shape((N_Y * N_MP, 8, HD))],
        [place, stack, small],
        scratch=[pltpu.VMEM((REPS * TILE, HD), F32)],
        smem=(0,),
        flops=10**9,
    )
    return part


def combine(packed, stack):
    (tile,) = call(
        combine_kernel,
        [shape((N_Z, TILE, HD), BF16)],
        [packed, stack],
        scratch=[pltpu.VMEM((REPS, HD), F32)],
        flops=10**8,
    )
    return tile


def per_device(
    query_raw, key_raw, values, decay_input, beta_input, log_rate, step_bias, gain, out_weight, upstream
):
    gain_row = gain[None, :]
    big = (key_raw, query_raw, values, upstream)
    rows = (decay_input.T, beta_input.T, log_rate[None, :], step_bias[None, :])
    tiles = forward(big, rows, gain_row)
    stack = lax.all_to_all(tiles, "dp", 0, 0)
    place = lax.axis_index("mp").astype(jnp.int32)[None]
    small = backward(place, (*big, out_weight), tiles, rows, gain_row)
    place = (lax.axis_index("dp") % N_Y).astype(jnp.int32)[None]
    part = gram(stack, small, place)
    part = lax.all_to_all(part, ("dp", "mp"), 0, 0, axis_index_groups=PLANES)
    (part,) = call(spread_kernel, [shape((N_Z, 8, HD))], [part])
    part = lax.all_to_all(part, "dp", 0, 0, axis_index_groups=Z_GROUPS)
    (part,) = call(gather_kernel, [shape((N_MP, 24, HD))], [part])
    packed = lax.all_to_all(part, "mp", 0, 0)
    whole = combine(packed, stack)
    whole = lax.all_to_all(whole, "dp", 0, 0, axis_index_groups=Z_GROUPS)
    (whole,) = call(unfold_kernel, [shape((N_Y, TILE, N_Z * HD), BF16)], [whole])
    whole = lax.all_to_all(whole, "dp", 0, 0, axis_index_groups=Y_GROUPS)
    gain_final, rate_final = call(trees_kernel, [shape((1, HD)), shape((1, HD))], [packed])
    return (
        whole.reshape(N_Y * TILE, N_Z * HD),
        gain_final[0],
        rate_final[0, : HEADS * N_MP],
    )


def solution(mesh):
    in_specs = (
        P("dp", "mp"),
        P("dp", "mp"),
        P("dp", "mp"),
        P("dp", "mp"),
        P("dp", "mp"),
        P("mp"),
        P("mp"),
        P(),
        P("mp", None),
        P("dp", None),
    )
    out_specs = (P("mp", None), P(), P())
    return jax.shard_map(
        per_device, mesh=mesh, in_specs=in_specs, out_specs=out_specs, check_vma=False
    )
```

time: 175 us -> 165 us (0.943)
  Pallas kernels: 11.2 us -> 19.8 us
  waiting for transfers between devices: 66 us -> 59.2 us
  blocking collectives: 67.5 us -> 61.2 us
  local copies, waits for them, and re-layouts: 5.69 us -> 1.49 us
    pallas_call x6 -> x8, Pallas kernels: 11.2 us -> 19.8 us  [call(): pl.pallas_call(body, out_shape=outs, in_specs=[pl.BlockSpec(memory_space=...]
    all_to_all x3, blocking collectives: 45.9 us -> 39.3 us  [the longest x1 16.6 us: per_device(): part = lax.all_to_all(part, 'dp', 0, 0, axis_index_groups=Z_GROUPS)]
    all_to_all x1, waiting for transfers between devices: 52.7 us -> 46.6 us  [per_device(): stack = lax.all_to_all(tiles, 'dp', 0, 0)]
    unnamed x23 -> x3, local copies, waits for them, and re-layouts: 3.9 us -> 0.97 us
  transfers between devices with their start and end apart: 2 -> 2, of which waited for: 2 -> 2; matrix products, arithmetic and copies ran while one was open for 0% -> 0% of each run, Pallas kernels for 1% -> 5%
where the time goes in v2:
time: 165 us; the launch traced here: 164 us
  blocking collectives  61.2 us (37%)
  waiting for transfers between devices  59.2 us (36%)
  starting transfers between devices  21.9 us (13%)
  Pallas kernels  19.8 us (12%)
    all_to_all x1, waiting for transfers between devices, per_device(): stack = lax.all_to_all(tiles, 'dp', 0, 0)  46.6 us
    all_to_all x1, blocking collectives, per_device(): whole = lax.all_to_all(whole, 'dp', 0, 0, axis_index_groups=Z_GROUPS)  21.9 us
    pallas_call x8, Pallas kernels, call(): pl.pallas_call(body, out_shape=outs, in_specs=[pl.BlockSpec(memory_space=...  19.8 us
    all_to_all x1, starting transfers between devices, per_device(): stack = lax.all_to_all(tiles, 'dp', 0, 0)  18.4 us
    all_to_all x1, blocking collectives, per_device(): part = lax.all_to_all(part, 'dp', 0, 0, axis_index_groups=Z_GROUPS)  16.6 us
    all_to_all x1, blocking collectives, per_device(): part = lax.all_to_all(part, ('dp', 'mp'), 0, 0, axis_index_groups=PLANES)  14.5 us
    all_to_all x1, waiting for transfers between devices, per_device(): whole = lax.all_to_all(whole, 'dp', 0, 0, axis_index_groups=Y_GROUPS)  12.6 us
    all_to_all x1, blocking collectives, per_device(): packed = lax.all_to_all(part, 'mp', 0, 0)  8.18 us
  transfers between devices with their start and end apart: 2, of which 2 were waited for; matrix products, arithmetic and copies ran while one was open for 0% of the time, Pallas kernels for 5%

profile of v2, /device:TPU:32, one launch (start us, length us, event | category | flops | bytes accessed | tf_op | source)
XLA Modules:
  0.0 164.4 jit_solution(1101104660202074872)
XLA Ops:
  0.6 6.8 %shard_map.121._ = bf16[64,64,128]{2,1,0:T(8,128)(2,1)} custom-call(bf16[128,128]{1,0:T(8,128)(2,1)} %k_any.3, bf16[128,128]{1,0:T(8,128)(2,1)} %q_any.3, bf16[128,256]{1,0:T(8,128)(2,1)} %v_any.3, bf16[128,2048]{1,0:T(8,128)(2,1)} %up_any.3, f32[2,128]{1,0:T(2,128)} %bitcast.12, f32[2,128]{1,0:T(2,128)} %bitcast.14, f32[1,2]{1,0:T(1,128)} %bitcast.16, ...), custom_call_target="tpu_custom_call" | custom-call | flops 2000000000 | bytes 1706512 | tf_op jit(solution)/shard_map/pallas_call | solution.py:278
  7.4 18.4 %all-to-all-start = ((bf16[64,64,128]{2,1,0:T(8,128)(2,1)}), bf16[64,64,128]{2,1,0:T(8,128)(2,1)S(1)}, u32[]{:S(2)}, u32[]{:S(2)}) async-start(bf16[64,64,128]{2,1,0:T(8,128)(2,1)} %shard_map.121._), calls=%async_computation | async-start | bytes 2097152 | tf_op jit(solution)/shard_map/all_to_all | solution.py:359
  25.8 7.5 %shard_map.122.small_ref = f32[2,128]{1,0:T(2,128)} custom-call(s32[1]{0:T(128)} %bitcast.6.place_ref, bf16[128,128]{1,0:T(8,128)(2,1)} %k_any.3, bf16[128,128]{1,0:T(8,128)(2,1)} %q_any.3, bf16[128,256]{1,0:T(8,128)(2,1)} %v_any.3, bf16[128,2048]{1,0:T(8,128)(2,1)} %up_any.3, bf16[256,2048]{1,0:T(8,128)(2,1)} %weight_any.1, ...), custom_call_target="tpu_custom_call" | custom-call | flops 2000000000 | bytes 2756116 | tf_op jit(solution)/shard_map/pallas_call | solution.py:278
  33.3 0.0 copy-start
  33.3 46.6 %all-to-all-done.x_ref = bf16[64,64,128]{2,1,0:T(8,128)(2,1)S(1)} async-done(((bf16[64,64,128]{2,1,0:T(8,128)(2,1)}), bf16[64,64,128]{2,1,0:T(8,128)(2,1)S(1)}, u32[]{:S(2)}, u32[]{:S(2)}) %all-to-all-start) | async-done | bytes 1048608 | tf_op jit(solution)/shard_map/all_to_all | solution.py:359
  79.9 0.0 copy-done
  79.9 1.7 %shard_map.123 = f32[32,8,128]{2,1,0:T(8,128)S(1)} custom-call(s32[1]{0:T(128)} %bitcast.place_ref, bf16[64,64,128]{2,1,0:T(8,128)(2,1)S(1)} %all-to-all-done.x_ref, f32[2,128]{1,0:T(2,128)S(1)} %copy-done), custom_call_target="tpu_custom_call" | custom-call | flops 1000000000 | bytes 1180676 | tf_op jit(solution)/shard_map/pallas_call | solution.py:278
  81.7 14.5 %all_to_all.30.in_ref = f32[32,8,128]{2,1,0:T(8,128)S(1)} all-to-all(f32[32,8,128]{2,1,0:T(8,128)S(1)} %shard_map.123), channel_id=1, replica_groups={{0,1,2,3,4,5,6,7,8,9,10,11,12,13,14,15,16,17,18,19,20,21,22,23,24,25,26..., dimensions={0} | all-to-all | bytes 262144 | tf_op jit(solution)/shard_map/all_to_all | solution.py:364
  96.2 16.6 %all_to_all.31.in_ref = f32[16,8,128]{2,1,0:T(8,128)S(1)} all-to-all(f32[16,8,128]{2,1,0:T(8,128)S(1)} %shard_map.124), channel_id=1, replica_groups={{0,32,64,96,128,160,192,224,256,288,320,352,384,416,448,480},{8,40,72,1..., dimensions={0} | all-to-all | bytes 131072 | tf_op jit(solution)/shard_map/all_to_all | solution.py:366
  112.9 8.2 %all_to_all.32.gram_ref.in_ref = f32[8,24,128]{2,1,0:T(8,128)S(1)} all-to-all(f32[8,24,128]{2,1,0:T(8,128)S(1)} %shard_map.125), channel_id=1, replica_groups=mesh['dp'=64,'mp'=8] {'mp'}, dimensions={0} | all-to-all | bytes 196608 | tf_op jit(solution)/shard_map/all_to_all | solution.py:368
  121.1 1.6 shard_map.126
  122.6 21.9 %all_to_all.33.in_ref = bf16[16,64,128]{2,1,0:T(8,128)(2,1)S(1)} all-to-all(bf16[16,64,128]{2,1,0:T(8,128)(2,1)S(1)} %shard_map.126), channel_id=1, replica_groups={{0,32,64,96,128,160,192,224,256,288,320,352,384,416,448,480},{8,40,72,1..., dimensions={0} | all-to-all | bytes 524288 | tf_op jit(solution)/shard_map/all_to_all | solution.py:370
  144.5 1.2 shard_map.127
  145.7 3.5 %all-to-all-start.5 = ((bf16[4,64,2048]{2,1,0:T(8,128)(2,1)}), bf16[4,64,2048]{2,1,0:T(8,128)(2,1)S(1)}, u32[]{:S(2)}, u32[]{:S(2)}) async-start(bf16[4,64,2048]{2,1,0:T(8,128)(2,1)} %shard_map.127), calls=%async_computation.5 | async-start | bytes 2097152 | tf_op jit(solution)/shard_map/all_to_all | solution.py:372
  149.2 1.1 shard_map.128
  150.3 0.5 slice_bitcast_fusion
  150.8 12.6 %all-to-all-done.5 = bf16[4,64,2048]{2,1,0:T(8,128)(2,1)S(1)} async-done(((bf16[4,64,2048]{2,1,0:T(8,128)(2,1)}), bf16[4,64,2048]{2,1,0:T(8,128)(2,1)S(1)}, u32[]{:S(2)}, u32[]{:S(2)}) %all-to-all-start.5) | async-done | bytes 1048608 | tf_op jit(solution)/shard_map/all_to_all | solution.py:372
  163.4 1.0 copy.14
  (2 shorter events, 0.1 us)
Async XLA Ops:
  7.4 72.5 %all-to-all-start = ((bf16[64,64,128]{2,1,0:T(8,128)(2,1)}), bf16[64,64,128]{2,1,0:T(8,128)(2,1)S(1)}, u32[]{:S(2)}, u32[]{:S(2)}) async-start(bf16[64,64,128]{2,1,0:T(8,128)(2,1)} %shard_map.121._), calls=%async_computation | async-start | bytes 2097152 | tf_op jit(solution)/shard_map/all_to_all | solution.py:359
  33.3 46.6 %copy-start = (f32[2,128]{1,0:T(2,128)S(1)}, f32[2,128]{1,0:T(2,128)}, u32[]{:S(2)}) copy-start(f32[2,128]{1,0:T(2,128)} %shard_map.122.small_ref) | copy-start | bytes 3076
  145.7 17.7 %all-to-all-start.5 = ((bf16[4,64,2048]{2,1,0:T(8,128)(2,1)}), bf16[4,64,2048]{2,1,0:T(8,128)(2,1)S(1)}, u32[]{:S(2)}, u32[]{:S(2)}) async-start(bf16[4,64,2048]{2,1,0:T(8,128)(2,1)} %shard_map.127), calls=%async_computation.5 | async-start | bytes 2097152 | tf_op jit(solution)/shard_map/all_to_all | solution.py:372

commit v3 on v2

--- a/solution.py
+++ b/solution.py
@@ -44,21 +44,33 @@
     return value / jnp.sqrt(jnp.sum(value * value, axis=-1, keepdims=True) + EPS)
 
 
-def invert_all(systems):
+def within(shift):
     row, col = places((TOK, TOK))
-    eye = (row == col).astype(F32)
-    close = (row >> 3) == (col >> 3)
-    first = [jnp.where(close, low, 0.0) for low in systems]
+    return (row >> shift) == (col >> shift)
+
+
+def invert_blocks(systems):
+    eye = within(0).astype(F32)
+    first = [jnp.where(within(3), low, 0.0) for low in systems]
     second = [matmul(a, a) for a in first]
+    out = [eye - a for a in first]
     fourth = [matmul(a, a) for a in second]
-    out = [eye - a for a in first]
     out = [a + matmul(a, b) for a, b in zip(out, second)]
-    out = [a + matmul(a, b) for a, b in zip(out, fourth)]
-    for shift in (3, 4, 5, 6):
-        off = ((row >> (shift + 1)) == (col >> (shift + 1))) & ((row >> shift) != (col >> shift))
-        parts = [matmul(jnp.where(off, low, 0.0), a) for low, a in zip(systems, out)]
-        out = [a - matmul(a, b) for a, b in zip(out, parts)]
-    return out
+    return [a + matmul(a, b) for a, b in zip(out, fourth)]
+
+
+def widen(systems, inverses, given, shift):
+    rest = within(shift + 2) & ~within(shift)
+    steps = [matmul(a, jnp.where(rest, low, 0.0)) for low, a in zip(systems, inverses)]
+    out = inverses if given is None else [matmul(a, v) for a, v in zip(inverses, given)]
+    squares = [matmul(a, a) for a in steps]
+    out = [v - matmul(a, v) for a, v in zip(steps, out)]
+    return [v + matmul(a, v) for a, v in zip(squares, out)]
+
+
+def solve_all(systems, given):
+    inverses = widen(systems, invert_blocks(systems), None, 3)
+    return widen(systems, inverses, given, 5)
 
 
 def small_inputs(dec_ref, beta_ref, rate_ref, bias_ref):
@@ -105,10 +117,9 @@
     fetches[1].wait()
     scores = matmul(unit_rows(q_ref[...]) * HD ** (-0.5), keys, NT)
     mixers, systems, _, strengths = delta_parts(cumul, beta, inner, scores)
-    inverses = invert_all(systems)
     fetches[2].wait()
     scaled = [strengths[h] * v_ref[:, h * HD : (h + 1) * HD].astype(F32) for h in heads]
-    writes = [matmul(inverses[h], scaled[h]) for h in heads]
+    writes = solve_all(systems, scaled)
     mixed = [matmul(mixers[h], writes[h]) for h in heads]
     normed = []
     for h in heads:
@@ -151,12 +162,10 @@
     scores = matmul(unit_rows(q_ref[...]) * HD ** (-0.5), keys, NT)
     cumul, beta = small_inputs(dec_ref, beta_ref, rate_ref, bias_ref)
     mixers, systems, spreads, strengths = delta_parts(cumul, beta, inner, scores)
-    inverses = invert_all(systems)
     scaled = [strengths[h] * v_ref[:, h * HD : (h + 1) * HD].astype(F32) for h in heads]
-    writes = [matmul(inverses[h], scaled[h]) for h in heads]
+    writes = solve_all(systems, scaled)
     outs = [matmul(mixers[h], writes[h]) for h in heads]
-    turns = [matmul(systems[h] * spreads[h], writes[h]) for h in heads]
-    turns = [matmul(inverses[h], turns[h]) for h in heads]
+    turns = solve_all(systems, [matmul(systems[h] * spreads[h], writes[h]) for h in heads])
     slopes = [
         matmul(mixers[h] * spreads[h], writes[h]) - matmul(mixers[h], turns[h]) for h in heads
     ]
@@ -175,6 +184,54 @@
     out_ref[...] = jnp.concatenate([grad_gain, rates], axis=0)
 
 
+def turn_rows(value, sign):
+    row, _ = places(value.shape)
+    parts = []
+    for g in range(REPS // 8):
+        part = value[8 * g : 8 * g + 8]
+        parts.append(pltpu.roll(part, (sign * 8 * g) % HD, 1) if g else part)
+    value = jnp.concatenate(parts, axis=0)
+    for bit in range(3):
+        value = jnp.where(
+            (row >> bit) & 1 == 1, pltpu.roll(value, (sign * 2**bit) % HD, 1), value
+        )
+    return value
+
+
+def twice(value):
+    return jnp.concatenate([value, value], axis=1)
+
+
+def pack_gram(total):
+    row, lane = places((REPS, HD))
+    wide = twice(total)
+    turned = turn_rows(wide, -1)
+    _, slot = places((16, HD))
+    packed = turned[0:16]
+    for q in range(1, 4):
+        packed = jnp.where(
+            slot >> 5 == q, pltpu.roll(turned[16 * q : 16 * q + 16], 32 * q, 1), packed
+        )
+    across = jnp.where(lane < REPS, (lane + 32) & (REPS - 1), lane - REPS)
+    return packed, jnp.sum(jnp.where(row == across, wide, 0.0), axis=0, keepdims=True)
+
+
+def unpack_gram(packed, last):
+    row, lane = places((REPS, HD))
+    turned = jnp.concatenate(
+        [packed] + [pltpu.roll(packed, HD - 32 * q, 1) for q in range(1, 4)], axis=0
+    )
+    upper = turn_rows(jnp.where(lane < 32, turned, 0.0), 1)
+    upper = upper + pltpu.roll(upper, REPS, 1)
+    col = lane & (REPS - 1)
+    other = jnp.where(row == col, 0.0, twice(upper[:, :REPS].T))
+    turned = pltpu.roll(last, REPS, 1)
+    half = jnp.where(lane[0:1] < REPS, last, turned)
+    rest = jnp.where(lane[0:1] < REPS, turned, last)
+    half = jnp.where(row == (col + 32) & (REPS - 1), half, 0.0)
+    return upper + other + half + jnp.where(row == col, rest, 0.0)
+
+
 def gram_kernel(place_ref, x_ref, small_ref, out_ref, wide):
     wide[...] = x_ref[...].astype(F32).reshape(REPS * TILE, HD)
     total = jnp.zeros((REPS, REPS), F32)
@@ -183,30 +240,34 @@
             [wide[pl.ds(f + e, REPS, stride=TILE), :].astype(BF16) for e in range(2)], axis=1
         )
         total = total + lax.dot_general(rows, rows, NT, preferred_element_type=F32)
-    half = jnp.concatenate([total[: REPS // 2], total[REPS // 2 :]], axis=1)
-    fill = jnp.zeros((3, HD), F32)
-    for m in range(N_MP):
-        kind, y = divmod(m, N_Y)
-        extra = jnp.where(place_ref[0] == y, small_ref[kind : kind + 1, :], 0.0)
-        block = jnp.concatenate([half[4 * m : 4 * m + 4], extra, fill], axis=0)
-        for target in range(N_Y):
-            out_ref[target * N_MP + m] = block
+    packed, last = pack_gram(total)
+    gain, rate = small_ref[0:1, :], small_ref[1:2, :]
+    own = [place_ref[0] == y for y in range(N_Y)]
+    rates = jnp.where(own[0], rate, 0.0)
+    for y in range(1, N_Y):
+        rates = jnp.where(own[y], pltpu.roll(rate, 16 * y, 1), rates)
+    gains = [jnp.where(own[y], gain, 0.0) for y in range(N_Y)]
+    block = jnp.concatenate([packed, last, rates, *gains, jnp.zeros((2, HD), F32)], axis=0)
+    out_ref[...] = jnp.broadcast_to(block[None], out_ref.shape)
+
+
+def split(value):
+    high = value.astype(BF16).astype(F32)
+    return high, value - high
 
 
 def spread_kernel(in_ref, out_ref):
     total = in_ref[0]
     for m in range(1, N_Y * N_MP):
         total = total + in_ref[m]
-    out_ref[...] = jnp.broadcast_to(total[None], out_ref.shape)
-
-
-def gather_kernel(in_ref, out_ref):
-    total = in_ref[0, 0:4]
-    for z in range(1, N_Z):
-        total = total + in_ref[z, 0:4]
-    fill = jnp.zeros((4, HD), F32)
-    block = jnp.concatenate([total, fill] + [in_ref[z, 4:5] for z in range(N_Z)], axis=0)
-    out_ref[...] = jnp.broadcast_to(block[None], out_ref.shape)
+    high, low = split(total)
+    lane = lax.broadcasted_iota(jnp.int32, (1, HD), 1)
+    last = jnp.where(lane < REPS, high[16:17], low[16:17])
+    rates = jnp.where(lane < REPS, high[17:18], pltpu.roll(low[17:18], REPS, 1))
+    block = jnp.concatenate(
+        [high[0:16], last, rates, high[18:22], low[18:22], jnp.zeros((6, HD), F32)], axis=0
+    )
+    out_ref[...] = jnp.broadcast_to(block.astype(BF16)[None], out_ref.shape)
 
 
 def small_tree(stack):
@@ -222,9 +283,17 @@
 
 
 def trees_kernel(in_ref, gain_ref, rate_ref):
-    for kind, out in enumerate((gain_ref, rate_ref)):
-        rows = [in_ref[kind * N_Y + r % N_Y, 8 + r // N_Y : 9 + r // N_Y, :] for r in range(REPS)]
-        out[...] = small_tree(jnp.concatenate(rows, axis=0))
+    lane = lax.broadcasted_iota(jnp.int32, (1, HD), 1)
+    gains, rates = [], []
+    for z in range(N_Z):
+        block = in_ref[z].astype(F32)
+        gains.append(block[18:22] + block[22:26])
+        row = block[17:18]
+        row = row + pltpu.roll(row, REPS, 1)
+        for y in range(N_Y):
+            rates.append(jnp.where(lane < 16, pltpu.roll(row, (-16 * y) % HD, 1), 0.0))
+    gain_ref[...] = small_tree(jnp.concatenate(gains, axis=0))
+    rate_ref[...] = small_tree(jnp.concatenate(rates, axis=0))
 
 
 def path_coefs(gram):
@@ -249,13 +318,11 @@
     return coefs
 
 
-def combine_kernel(gram_ref, x_ref, out_ref, factor):
-    lane = lax.broadcasted_iota(jnp.int32, (REPS // 2, HD), 1)
-    packed = jnp.concatenate([gram_ref[m, 0:4] for m in range(N_MP)], axis=0)
-    turned = pltpu.roll(packed, REPS, 1)
-    gram = jnp.concatenate(
-        [jnp.where(lane < REPS, packed, turned), jnp.where(lane < REPS, turned, packed)], axis=0
-    )
+def combine_kernel(in_ref, x_ref, out_ref, factor):
+    total = in_ref[0].astype(F32)
+    for z in range(1, N_Z):
+        total = total + in_ref[z].astype(F32)
+    gram = unpack_gram(total[0:16], total[16:17])
     factor[...] = jnp.broadcast_to(path_coefs(gram), (REPS, HD))
     total = jnp.zeros((TILE, HD), F32)
     for r in range(REPS):
@@ -329,7 +396,7 @@
 def gram(stack, small, place):
     (part,) = call(
         gram_kernel,
-        [shape((N_Y * N_MP, 8, HD))],
+        [shape((N_Y * N_MP, 24, HD))],
         [place, stack, small],
         scratch=[pltpu.VMEM((REPS * TILE, HD), F32)],
         smem=(0,),
@@ -362,10 +429,8 @@
     place = (lax.axis_index("dp") % N_Y).astype(jnp.int32)[None]
     part = gram(stack, small, place)
     part = lax.all_to_all(part, ("dp", "mp"), 0, 0, axis_index_groups=PLANES)
-    (part,) = call(spread_kernel, [shape((N_Z, 8, HD))], [part])
-    part = lax.all_to_all(part, "dp", 0, 0, axis_index_groups=Z_GROUPS)
-    (part,) = call(gather_kernel, [shape((N_MP, 24, HD))], [part])
-    packed = lax.all_to_all(part, "mp", 0, 0)
+    (part,) = call(spread_kernel, [shape((N_Z, 32, HD), BF16)], [part])
+    packed = lax.all_to_all(part, "dp", 0, 0, axis_index_groups=Z_GROUPS)
     whole = combine(packed, stack)
     whole = lax.all_to_all(whole, "dp", 0, 0, axis_index_groups=Z_GROUPS)
     (whole,) = call(unfold_kernel, [shape((N_Y, TILE, N_Z * HD), BF16)], [whole])

time: 165 us -> 163 us (0.988)
  blocking collectives: 61.2 us -> 57.8 us
    all_to_all x2 -> x1, blocking collectives: 24.8 us -> 18.7 us  [per_device(): packed = lax.all_to_all(part, 'dp', 0, 0, axis_index_groups=Z_GROUPS)]
    all_to_all x1, blocking collectives: 14.5 us -> 17 us  [per_device(): part = lax.all_to_all(part, ('dp', 'mp'), 0, 0, axis_index_groups=PLANES)]
    pallas_call x8 -> x7, Pallas kernels: 19.8 us -> 20.7 us  [call(): pl.pallas_call(body, out_shape=outs, in_specs=[pl.BlockSpec(memory_space=...]
where the time goes in v3:
time: 163 us; the launch traced here: 162 us
  waiting for transfers between devices  59.6 us (37%)
  blocking collectives  57.8 us (35%)
  starting transfers between devices  21.9 us (13%)
  Pallas kernels  20.7 us (13%)
    all_to_all x1, waiting for transfers between devices, per_device(): stack = lax.all_to_all(tiles, 'dp', 0, 0)  46.6 us
    all_to_all x1, blocking collectives, per_device(): whole = lax.all_to_all(whole, 'dp', 0, 0, axis_index_groups=Z_GROUPS)  22.1 us
    pallas_call x7, Pallas kernels, call(): pl.pallas_call(body, out_shape=outs, in_specs=[pl.BlockSpec(memory_space=...  20.7 us
    all_to_all x1, blocking collectives, per_device(): packed = lax.all_to_all(part, 'dp', 0, 0, axis_index_groups=Z_GROUPS)  18.7 us
    all_to_all x1, starting transfers between devices, per_device(): stack = lax.all_to_all(tiles, 'dp', 0, 0)  18.4 us
    all_to_all x1, blocking collectives, per_device(): part = lax.all_to_all(part, ('dp', 'mp'), 0, 0, axis_index_groups=PLANES)  17 us
    all_to_all x1, waiting for transfers between devices, per_device(): whole = lax.all_to_all(whole, 'dp', 0, 0, axis_index_groups=Y_GROUPS)  13 us
    all_to_all x1, starting transfers between devices, per_device(): whole = lax.all_to_all(whole, 'dp', 0, 0, axis_index_groups=Y_GROUPS)  3.52 us
  transfers between devices with their start and end apart: 2, of which 2 were waited for; matrix products, arithmetic and copies ran while one was open for 0% of the time, Pallas kernels for 5%

profile of v3, /device:TPU:32, one launch (start us, length us, event | category | flops | bytes accessed | tf_op | source)
XLA Modules:
  0.0 162.2 jit_solution(9329602554672946342)
XLA Ops:
  0.6 6.6 %shard_map.121._ = bf16[64,64,128]{2,1,0:T(8,128)(2,1)} custom-call(bf16[128,128]{1,0:T(8,128)(2,1)} %k_any.3, bf16[128,128]{1,0:T(8,128)(2,1)} %q_any.3, bf16[128,256]{1,0:T(8,128)(2,1)} %v_any.3, bf16[128,2048]{1,0:T(8,128)(2,1)} %up_any.3, f32[2,128]{1,0:T(2,128)} %bitcast.12, f32[2,128]{1,0:T(2,128)} %bitcast.14, f32[1,2]{1,0:T(1,128)} %bitcast.16, ...), custom_call_target="tpu_custom_call" | custom-call | flops 2000000000 | bytes 1706512 | tf_op jit(solution)/shard_map/pallas_call | solution.py:345
  7.2 18.4 %all-to-all-start = ((bf16[64,64,128]{2,1,0:T(8,128)(2,1)}), bf16[64,64,128]{2,1,0:T(8,128)(2,1)S(1)}, u32[]{:S(2)}, u32[]{:S(2)}) async-start(bf16[64,64,128]{2,1,0:T(8,128)(2,1)} %shard_map.121._), calls=%async_computation | async-start | bytes 2097152 | tf_op jit(solution)/shard_map/all_to_all | solution.py:426
  25.6 7.5 %shard_map.122.small_ref = f32[2,128]{1,0:T(2,128)} custom-call(s32[1]{0:T(128)} %bitcast.6.place_ref, bf16[128,128]{1,0:T(8,128)(2,1)} %k_any.3, bf16[128,128]{1,0:T(8,128)(2,1)} %q_any.3, bf16[128,256]{1,0:T(8,128)(2,1)} %v_any.3, bf16[128,2048]{1,0:T(8,128)(2,1)} %up_any.3, bf16[256,2048]{1,0:T(8,128)(2,1)} %weight_any.1, ...), custom_call_target="tpu_custom_call" | custom-call | flops 2000000000 | bytes 2756116 | tf_op jit(solution)/shard_map/pallas_call | solution.py:345
  33.1 0.0 copy-start
  33.1 46.6 %all-to-all-done.x_ref = bf16[64,64,128]{2,1,0:T(8,128)(2,1)S(1)} async-done(((bf16[64,64,128]{2,1,0:T(8,128)(2,1)}), bf16[64,64,128]{2,1,0:T(8,128)(2,1)S(1)}, u32[]{:S(2)}, u32[]{:S(2)}) %all-to-all-start) | async-done | bytes 1048608 | tf_op jit(solution)/shard_map/all_to_all | solution.py:426
  79.7 0.0 copy-done
  79.7 2.1 %shard_map.123 = f32[32,24,128]{2,1,0:T(8,128)S(1)} custom-call(s32[1]{0:T(128)} %bitcast.place_ref, bf16[64,64,128]{2,1,0:T(8,128)(2,1)S(1)} %all-to-all-done.x_ref, f32[2,128]{1,0:T(2,128)S(1)} %copy-done), custom_call_target="tpu_custom_call" | custom-call | flops 1000000000 | bytes 1442820 | tf_op jit(solution)/shard_map/pallas_call | solution.py:345
  81.8 17.0 %all_to_all.25.in_ref = f32[32,24,128]{2,1,0:T(8,128)S(1)} all-to-all(f32[32,24,128]{2,1,0:T(8,128)S(1)} %shard_map.123), channel_id=1, replica_groups={{0,1,2,3,4,5,6,7,8,9,10,11,12,13,14,15,16,17,18,19,20,21,22,23,24,25,26..., dimensions={0} | all-to-all | bytes 786432 | tf_op jit(solution)/shard_map/all_to_all | solution.py:431
  98.8 0.1 shard_map.124
  99.0 18.7 %all_to_all.26.in_ref = bf16[16,32,128]{2,1,0:T(8,128)(2,1)S(1)} all-to-all(bf16[16,32,128]{2,1,0:T(8,128)(2,1)S(1)} %shard_map.124), channel_id=1, replica_groups={{0,32,64,96,128,160,192,224,256,288,320,352,384,416,448,480},{8,40,72,1..., dimensions={0} | all-to-all | bytes 262144 | tf_op jit(solution)/shard_map/all_to_all | solution.py:433
  117.6 2.1 %shard_map.125 = bf16[16,64,128]{2,1,0:T(8,128)(2,1)S(1)} custom-call(bf16[16,32,128]{2,1,0:T(8,128)(2,1)S(1)} %all_to_all.26.in_ref, bf16[64,64,128]{2,1,0:T(8,128)(2,1)S(1)} %all-to-all-done.x_ref), custom_call_target="tpu_custom_call" | custom-call | flops 100000000 | bytes 1441792 | tf_op jit(solution)/shard_map/pallas_call | solution.py:345
  119.7 22.1 %all_to_all.27.in_ref = bf16[16,64,128]{2,1,0:T(8,128)(2,1)S(1)} all-to-all(bf16[16,64,128]{2,1,0:T(8,128)(2,1)S(1)} %shard_map.125), channel_id=1, replica_groups={{0,32,64,96,128,160,192,224,256,288,320,352,384,416,448,480},{8,40,72,1..., dimensions={0} | all-to-all | bytes 524288 | tf_op jit(solution)/shard_map/all_to_all | solution.py:435
  141.8 1.2 shard_map.126
  143.0 3.5 %all-to-all-start.4 = ((bf16[4,64,2048]{2,1,0:T(8,128)(2,1)}), bf16[4,64,2048]{2,1,0:T(8,128)(2,1)S(1)}, u32[]{:S(2)}, u32[]{:S(2)}) async-start(bf16[4,64,2048]{2,1,0:T(8,128)(2,1)} %shard_map.126), calls=%async_computation.4 | async-start | bytes 2097152 | tf_op jit(solution)/shard_map/all_to_all | solution.py:437
  146.5 1.2 shard_map.127
  147.8 0.5 slice_bitcast_fusion
  148.3 13.0 %all-to-all-done.4 = bf16[4,64,2048]{2,1,0:T(8,128)(2,1)S(1)} async-done(((bf16[4,64,2048]{2,1,0:T(8,128)(2,1)}), bf16[4,64,2048]{2,1,0:T(8,128)(2,1)S(1)}, u32[]{:S(2)}, u32[]{:S(2)}) %all-to-all-start.4) | async-done | bytes 1048608 | tf_op jit(solution)/shard_map/all_to_all | solution.py:437
  161.2 1.0 copy.14
Async XLA Ops:
  7.2 72.5 %all-to-all-start = ((bf16[64,64,128]{2,1,0:T(8,128)(2,1)}), bf16[64,64,128]{2,1,0:T(8,128)(2,1)S(1)}, u32[]{:S(2)}, u32[]{:S(2)}) async-start(bf16[64,64,128]{2,1,0:T(8,128)(2,1)} %shard_map.121._), calls=%async_computation | async-start | bytes 2097152 | tf_op jit(solution)/shard_map/all_to_all | solution.py:426
  33.1 46.6 %copy-start = (f32[2,128]{1,0:T(2,128)S(1)}, f32[2,128]{1,0:T(2,128)}, u32[]{:S(2)}) copy-start(f32[2,128]{1,0:T(2,128)} %shard_map.122.small_ref) | copy-start | bytes 3076
  143.0 18.2 %all-to-all-start.4 = ((bf16[4,64,2048]{2,1,0:T(8,128)(2,1)}), bf16[4,64,2048]{2,1,0:T(8,128)(2,1)S(1)}, u32[]{:S(2)}, u32[]{:S(2)}) async-start(bf16[4,64,2048]{2,1,0:T(8,128)(2,1)} %shard_map.126), calls=%async_computation.4 | async-start | bytes 2097152 | tf_op jit(solution)/shard_map/all_to_all | solution.py:437

commit v4 on v3

--- a/solution.py
+++ b/solution.py
@@ -32,6 +32,13 @@
     return lax.dot_general(a, b, dims, precision=HIGH, preferred_element_type=F32)
 
 
+def matmul3(a, b, dims=NN):
+    ah, bh = a.astype(BF16), b.astype(BF16)
+    al, bl = (a - ah.astype(F32)).astype(BF16), (b - bh.astype(F32)).astype(BF16)
+    dot = functools.partial(lax.dot_general, dimension_numbers=dims, preferred_element_type=F32)
+    return dot(ah, bh) + (dot(ah, bl) + dot(al, bh))
+
+
 def places(shape):
     return (
         lax.broadcasted_iota(jnp.int32, shape, 0),
@@ -49,28 +56,28 @@
     return (row >> shift) == (col >> shift)
 
 
-def invert_blocks(systems):
+def invert_blocks(systems, mul):
     eye = within(0).astype(F32)
     first = [jnp.where(within(3), low, 0.0) for low in systems]
-    second = [matmul(a, a) for a in first]
+    second = [mul(a, a) for a in first]
     out = [eye - a for a in first]
-    fourth = [matmul(a, a) for a in second]
-    out = [a + matmul(a, b) for a, b in zip(out, second)]
-    return [a + matmul(a, b) for a, b in zip(out, fourth)]
-
-
-def widen(systems, inverses, given, shift):
+    fourth = [mul(a, a) for a in second]
+    out = [a + mul(a, b) for a, b in zip(out, second)]
+    return [a + mul(a, b) for a, b in zip(out, fourth)]
+
+
+def widen(systems, inverses, given, shift, mul):
     rest = within(shift + 2) & ~within(shift)
-    steps = [matmul(a, jnp.where(rest, low, 0.0)) for low, a in zip(systems, inverses)]
-    out = inverses if given is None else [matmul(a, v) for a, v in zip(inverses, given)]
-    squares = [matmul(a, a) for a in steps]
-    out = [v - matmul(a, v) for a, v in zip(steps, out)]
-    return [v + matmul(a, v) for a, v in zip(squares, out)]
-
-
-def solve_all(systems, given):
-    inverses = widen(systems, invert_blocks(systems), None, 3)
-    return widen(systems, inverses, given, 5)
+    steps = [mul(a, jnp.where(rest, low, 0.0)) for low, a in zip(systems, inverses)]
+    out = inverses if given is None else [mul(a, v) for a, v in zip(inverses, given)]
+    squares = [mul(a, a) for a in steps]
+    out = [v - mul(a, v) for a, v in zip(steps, out)]
+    return [v + mul(a, v) for a, v in zip(squares, out)]
+
+
+def solve_all(systems, given, mul=matmul):
+    inverses = widen(systems, invert_blocks(systems, mul), None, 3, mul)
+    return widen(systems, inverses, given, 5, mul)
 
 
 def small_inputs(dec_ref, beta_ref, rate_ref, bias_ref):
@@ -113,14 +120,14 @@
     heads = range(HEADS)
     fetches[0].wait()
     keys = unit_rows(k_ref[...])
-    inner = matmul(keys, keys, NT)
+    inner = matmul3(keys, keys, NT)
     fetches[1].wait()
-    scores = matmul(unit_rows(q_ref[...]) * HD ** (-0.5), keys, NT)
+    scores = matmul3(unit_rows(q_ref[...]) * HD ** (-0.5), keys, NT)
     mixers, systems, _, strengths = delta_parts(cumul, beta, inner, scores)
     fetches[2].wait()
     scaled = [strengths[h] * v_ref[:, h * HD : (h + 1) * HD].astype(F32) for h in heads]
-    writes = solve_all(systems, scaled)
-    mixed = [matmul(mixers[h], writes[h]) for h in heads]
+    writes = solve_all(systems, scaled, matmul3)
+    mixed = [matmul3(mixers[h], writes[h]) for h in heads]
     normed = []
     for h in heads:
         scale = lax.rsqrt(jnp.mean(mixed[h] * mixed[h], axis=-1, keepdims=True) + EPS)
@@ -184,18 +191,24 @@
     out_ref[...] = jnp.concatenate([grad_gain, rates], axis=0)
 
 
-def turn_rows(value, sign):
+def turn_left(value):
     row, _ = places(value.shape)
     parts = []
     for g in range(REPS // 8):
         part = value[8 * g : 8 * g + 8]
-        parts.append(pltpu.roll(part, (sign * 8 * g) % HD, 1) if g else part)
+        parts.append(pltpu.roll(part, HD - 8 * g, 1) if g else part)
     value = jnp.concatenate(parts, axis=0)
     for bit in range(3):
-        value = jnp.where(
-            (row >> bit) & 1 == 1, pltpu.roll(value, (sign * 2**bit) % HD, 1), value
-        )
+        value = jnp.where((row >> bit) & 1 == 1, pltpu.roll(value, HD - 2**bit, 1), value)
     return value
+
+
+def turn_right(value):
+    parts = [
+        pltpu.roll(value[8 * g : 8 * g + 8], 8 * g, 1, stride=1, stride_axis=0)
+        for g in range(REPS // 8)
+    ]
+    return jnp.concatenate(parts, axis=0)
 
 
 def twice(value):
@@ -205,15 +218,15 @@
 def pack_gram(total):
     row, lane = places((REPS, HD))
     wide = twice(total)
-    turned = turn_rows(wide, -1)
+    turned = turn_left(wide)
     _, slot = places((16, HD))
     packed = turned[0:16]
     for q in range(1, 4):
         packed = jnp.where(
             slot >> 5 == q, pltpu.roll(turned[16 * q : 16 * q + 16], 32 * q, 1), packed
         )
-    across = jnp.where(lane < REPS, (lane + 32) & (REPS - 1), lane - REPS)
-    return packed, jnp.sum(jnp.where(row == across, wide, 0.0), axis=0, keepdims=True)
+    across = (lane < REPS) & (row == (lane + 32) & (REPS - 1))
+    return packed, jnp.sum(jnp.where(across, wide, 0.0), axis=0, keepdims=True)
 
 
 def unpack_gram(packed, last):
@@ -221,15 +234,12 @@
     turned = jnp.concatenate(
         [packed] + [pltpu.roll(packed, HD - 32 * q, 1) for q in range(1, 4)], axis=0
     )
-    upper = turn_rows(jnp.where(lane < 32, turned, 0.0), 1)
+    upper = turn_right(jnp.where(lane < 32, turned, 0.0))
     upper = upper + pltpu.roll(upper, REPS, 1)
     col = lane & (REPS - 1)
     other = jnp.where(row == col, 0.0, twice(upper[:, :REPS].T))
-    turned = pltpu.roll(last, REPS, 1)
-    half = jnp.where(lane[0:1] < REPS, last, turned)
-    rest = jnp.where(lane[0:1] < REPS, turned, last)
-    half = jnp.where(row == (col + 32) & (REPS - 1), half, 0.0)
-    return upper + other + half + jnp.where(row == col, rest, 0.0)
+    half = last + pltpu.roll(last, REPS, 1)
+    return upper + other + jnp.where(row == (col + 32) & (REPS - 1), half, 0.0)
 
 
 def gram_kernel(place_ref, x_ref, small_ref, out_ref, wide):
@@ -241,14 +251,15 @@
         )
         total = total + lax.dot_general(rows, rows, NT, preferred_element_type=F32)
     packed, last = pack_gram(total)
-    gain, rate = small_ref[0:1, :], small_ref[1:2, :]
     own = [place_ref[0] == y for y in range(N_Y)]
+    high, low = split(small_ref[...])
+    rate = high[1:2] + pltpu.roll(low[1:2], REPS, 1)
     rates = jnp.where(own[0], rate, 0.0)
     for y in range(1, N_Y):
         rates = jnp.where(own[y], pltpu.roll(rate, 16 * y, 1), rates)
-    gains = [jnp.where(own[y], gain, 0.0) for y in range(N_Y)]
-    block = jnp.concatenate([packed, last, rates, *gains, jnp.zeros((2, HD), F32)], axis=0)
-    out_ref[...] = jnp.broadcast_to(block[None], out_ref.shape)
+    gains = [jnp.where(own[y], part[0:1], 0.0) for part in (high, low) for y in range(N_Y)]
+    block = jnp.concatenate([packed, last, rates, *gains, jnp.zeros((6, HD), F32)], axis=0)
+    out_ref[...] = jnp.broadcast_to(block.astype(BF16)[None], out_ref.shape)
 
 
 def split(value):
@@ -257,15 +268,15 @@
 
 
 def spread_kernel(in_ref, out_ref):
-    total = in_ref[0]
+    total = in_ref[0].astype(F32)
     for m in range(1, N_Y * N_MP):
-        total = total + in_ref[m]
-    high, low = split(total)
+        total = total + in_ref[m].astype(F32)
     lane = lax.broadcasted_iota(jnp.int32, (1, HD), 1)
-    last = jnp.where(lane < REPS, high[16:17], low[16:17])
-    rates = jnp.where(lane < REPS, high[17:18], pltpu.roll(low[17:18], REPS, 1))
+    rates = total[17:18] + pltpu.roll(total[17:18], REPS, 1)
+    high, low = split(jnp.concatenate([rates, total[18:22] + total[22:26]], axis=0))
+    rates = jnp.where(lane < REPS, high[0:1], low[0:1])
     block = jnp.concatenate(
-        [high[0:16], last, rates, high[18:22], low[18:22], jnp.zeros((6, HD), F32)], axis=0
+        [total[0:17], rates, high[1:5], low[1:5], jnp.zeros((6, HD), F32)], axis=0
     )
     out_ref[...] = jnp.broadcast_to(block.astype(BF16)[None], out_ref.shape)
 
@@ -298,18 +309,22 @@
 
 def path_coefs(gram):
     row, lane = places((REPS, HD))
-    same = row == (lane & (REPS - 1))
-    near = row == lane
+    col = lane & (REPS - 1)
+    first = lane < REPS
+
+    def ratio(inner, norm):
+        return 1.0 - inner / (2.0 * (norm + EPS))
+
+    def pick(mask, axis):
+        return jnp.sum(jnp.where(mask, gram, 0.0), axis=axis, keepdims=True)
+
     coefs = jnp.ones((REPS, 1), F32)
     half = REPS // 2
+    same = row == col
     while half:
-        other = pltpu.roll(gram, half, 1)
-        norm_col = jnp.sum(jnp.where(near, gram, 0.0), axis=1, keepdims=True)
-        inner_col = jnp.sum(jnp.where(near, other, 0.0), axis=1, keepdims=True)
-        norm_row = jnp.sum(jnp.where(same, gram, 0.0), axis=0, keepdims=True)
-        inner_row = jnp.sum(jnp.where(same, other, 0.0), axis=0, keepdims=True)
-        by_col = 1.0 - inner_col / (2.0 * (norm_col + EPS))
-        by_row = 1.0 - inner_row / (2.0 * (norm_row + EPS))
+        across = row == (col + half) & (REPS - 1)
+        by_col = ratio(pick(across & first, 1), pick(same & first, 1))
+        by_row = ratio(pick(across, 0), pick(same, 0))
         coefs = coefs * by_col
         part = by_col * by_row * gram
         part = part + pltpu.roll(part, half, 1)
@@ -396,7 +411,7 @@
 def gram(stack, small, place):
     (part,) = call(
         gram_kernel,
-        [shape((N_Y * N_MP, 24, HD))],
+        [shape((N_Y * N_MP, 32, HD), BF16)],
         [place, stack, small],
         scratch=[pltpu.VMEM((REPS * TILE, HD), F32)],
         smem=(0,),
@@ -435,7 +450,9 @@
     whole = lax.all_to_all(whole, "dp", 0, 0, axis_index_groups=Z_GROUPS)
     (whole,) = call(unfold_kernel, [shape((N_Y, TILE, N_Z * HD), BF16)], [whole])
     whole = lax.all_to_all(whole, "dp", 0, 0, axis_index_groups=Y_GROUPS)
-    gain_final, rate_final = call(trees_kernel, [shape((1, HD)), shape((1, HD))], [packed])
+    gain_final, rate_final = call(
+        trees_kernel, [shape((1, HD)), shape((1, HD))], [packed]
+    )
     return (
         whole.reshape(N_Y * TILE, N_Z * HD),
         gain_final[0],

time: 163 us -> 160 us (0.982)
  no operation moved by 1% of the time
where the time goes in v4:
time: 160 us
  waiting for transfers between devices  59.5 us (37%)
  blocking collectives  57.1 us (36%)
  starting transfers between devices  21.9 us (14%)
  Pallas kernels  19.1 us (12%)
    all_to_all x1, waiting for transfers between devices, per_device(): stack = lax.all_to_all(tiles, 'dp', 0, 0)  46.6 us
    all_to_all x1, blocking collectives, per_device(): whole = lax.all_to_all(whole, 'dp', 0, 0, axis_index_groups=Z_GROUPS)  22.7 us
    pallas_call x7, Pallas kernels, call(): pl.pallas_call(body, out_shape=outs, in_specs=[pl.BlockSpec(memory_space=...  19.1 us
    all_to_all x1, blocking collectives, per_device(): packed = lax.all_to_all(part, 'dp', 0, 0, axis_index_groups=Z_GROUPS)  18.8 us
    all_to_all x1, starting transfers between devices, per_device(): stack = lax.all_to_all(tiles, 'dp', 0, 0)  18.4 us
    all_to_all x1, blocking collectives, per_device(): part = lax.all_to_all(part, ('dp', 'mp'), 0, 0, axis_index_groups=PLANES)  15.6 us
    all_to_all x1, waiting for transfers between devices, per_device(): whole = lax.all_to_all(whole, 'dp', 0, 0, axis_index_groups=Y_GROUPS)  12.8 us
    all_to_all x1, starting transfers between devices, per_device(): whole = lax.all_to_all(whole, 'dp', 0, 0, axis_index_groups=Y_GROUPS)  3.52 us
  transfers between devices with their start and end apart: 2, of which 2 were waited for; matrix products, arithmetic and copies ran while one was open for 0% of the time, Pallas kernels for 5%

profile of v4, /device:TPU:32, one launch (start us, length us, event | category | flops | bytes accessed | tf_op | source)
XLA Modules:
  0.0 159.8 jit_solution(4638358988796448699)
XLA Ops:
  0.6 5.5 %shard_map.121._ = bf16[64,64,128]{2,1,0:T(8,128)(2,1)} custom-call(bf16[128,128]{1,0:T(8,128)(2,1)} %k_any.3, bf16[128,128]{1,0:T(8,128)(2,1)} %q_any.3, bf16[128,256]{1,0:T(8,128)(2,1)} %v_any.3, bf16[128,2048]{1,0:T(8,128)(2,1)} %up_any.3, f32[2,128]{1,0:T(2,128)} %bitcast.12, f32[2,128]{1,0:T(2,128)} %bitcast.14, f32[1,2]{1,0:T(1,128)} %bitcast.16, ...), custom_call_target="tpu_custom_call" | custom-call | flops 2000000000 | bytes 1706512 | tf_op jit(solution)/shard_map/pallas_call | solution.py:360
  6.2 18.4 %all-to-all-start = ((bf16[64,64,128]{2,1,0:T(8,128)(2,1)}), bf16[64,64,128]{2,1,0:T(8,128)(2,1)S(1)}, u32[]{:S(2)}, u32[]{:S(2)}) async-start(bf16[64,64,128]{2,1,0:T(8,128)(2,1)} %shard_map.121._), calls=%async_computation | async-start | bytes 2097152 | tf_op jit(solution)/shard_map/all_to_all | solution.py:441
  24.6 7.5 %shard_map.122.small_ref = f32[2,128]{1,0:T(2,128)} custom-call(s32[1]{0:T(128)} %bitcast.6.place_ref, bf16[128,128]{1,0:T(8,128)(2,1)} %k_any.3, bf16[128,128]{1,0:T(8,128)(2,1)} %q_any.3, bf16[128,256]{1,0:T(8,128)(2,1)} %v_any.3, bf16[128,2048]{1,0:T(8,128)(2,1)} %up_any.3, bf16[256,2048]{1,0:T(8,128)(2,1)} %weight_any.1, ...), custom_call_target="tpu_custom_call" | custom-call | flops 2000000000 | bytes 2756116 | tf_op jit(solution)/shard_map/pallas_call | solution.py:360
  32.1 0.0 copy-start
  32.1 46.6 %all-to-all-done.x_ref = bf16[64,64,128]{2,1,0:T(8,128)(2,1)S(1)} async-done(((bf16[64,64,128]{2,1,0:T(8,128)(2,1)}), bf16[64,64,128]{2,1,0:T(8,128)(2,1)S(1)}, u32[]{:S(2)}, u32[]{:S(2)}) %all-to-all-start) | async-done | bytes 1048608 | tf_op jit(solution)/shard_map/all_to_all | solution.py:441
  78.7 0.0 copy-done
  78.7 2.1 %shard_map.123 = bf16[32,32,128]{2,1,0:T(8,128)(2,1)S(1)} custom-call(s32[1]{0:T(128)} %bitcast.place_ref, bf16[64,64,128]{2,1,0:T(8,128)(2,1)S(1)} %all-to-all-done.x_ref, f32[2,128]{1,0:T(2,128)S(1)} %copy-done), custom_call_target="tpu_custom_call" | custom-call | flops 1000000000 | bytes 1311748 | tf_op jit(solution)/shard_map/pallas_call | solution.py:360
  80.8 15.6 %all_to_all.25.in_ref = bf16[32,32,128]{2,1,0:T(8,128)(2,1)S(1)} all-to-all(bf16[32,32,128]{2,1,0:T(8,128)(2,1)S(1)} %shard_map.123), channel_id=1, replica_groups={{0,1,2,3,4,5,6,7,8,9,10,11,12,13,14,15,16,17,18,19,20,21,22,23,24,25,26..., dimensions={0} | all-to-all | bytes 524288 | tf_op jit(solution)/shard_map/all_to_all | solution.py:446
  96.4 0.1 shard_map.124
  96.5 18.8 %all_to_all.26.in_ref = bf16[16,32,128]{2,1,0:T(8,128)(2,1)S(1)} all-to-all(bf16[16,32,128]{2,1,0:T(8,128)(2,1)S(1)} %shard_map.124), channel_id=1, replica_groups={{0,32,64,96,128,160,192,224,256,288,320,352,384,416,448,480},{8,40,72,1..., dimensions={0} | all-to-all | bytes 262144 | tf_op jit(solution)/shard_map/all_to_all | solution.py:448
  115.3 1.5 shard_map.125
  116.8 22.7 %all_to_all.27.in_ref = bf16[16,64,128]{2,1,0:T(8,128)(2,1)S(1)} all-to-all(bf16[16,64,128]{2,1,0:T(8,128)(2,1)S(1)} %shard_map.125), channel_id=1, replica_groups={{0,32,64,96,128,160,192,224,256,288,320,352,384,416,448,480},{8,40,72,1..., dimensions={0} | all-to-all | bytes 524288 | tf_op jit(solution)/shard_map/all_to_all | solution.py:450
  139.5 1.2 shard_map.126
  140.7 3.5 %all-to-all-start.4 = ((bf16[4,64,2048]{2,1,0:T(8,128)(2,1)}), bf16[4,64,2048]{2,1,0:T(8,128)(2,1)S(1)}, u32[]{:S(2)}, u32[]{:S(2)}) async-start(bf16[4,64,2048]{2,1,0:T(8,128)(2,1)} %shard_map.126), calls=%async_computation.4 | async-start | bytes 2097152 | tf_op jit(solution)/shard_map/all_to_all | solution.py:452
  144.2 1.2 shard_map.127
  145.5 0.5 slice_bitcast_fusion
  146.0 12.8 %all-to-all-done.4 = bf16[4,64,2048]{2,1,0:T(8,128)(2,1)S(1)} async-done(((bf16[4,64,2048]{2,1,0:T(8,128)(2,1)}), bf16[4,64,2048]{2,1,0:T(8,128)(2,1)S(1)}, u32[]{:S(2)}, u32[]{:S(2)}) %all-to-all-start.4) | async-done | bytes 1048608 | tf_op jit(solution)/shard_map/all_to_all | solution.py:452
  158.8 1.0 copy.14
Async XLA Ops:
  6.2 72.5 %all-to-all-start = ((bf16[64,64,128]{2,1,0:T(8,128)(2,1)}), bf16[64,64,128]{2,1,0:T(8,128)(2,1)S(1)}, u32[]{:S(2)}, u32[]{:S(2)}) async-start(bf16[64,64,128]{2,1,0:T(8,128)(2,1)} %shard_map.121._), calls=%async_computation | async-start | bytes 2097152 | tf_op jit(solution)/shard_map/all_to_all | solution.py:441
  32.1 46.6 %copy-start = (f32[2,128]{1,0:T(2,128)S(1)}, f32[2,128]{1,0:T(2,128)}, u32[]{:S(2)}) copy-start(f32[2,128]{1,0:T(2,128)} %shard_map.122.small_ref) | copy-start | bytes 3076
  140.7 18.1 %all-to-all-start.4 = ((bf16[4,64,2048]{2,1,0:T(8,128)(2,1)}), bf16[4,64,2048]{2,1,0:T(8,128)(2,1)S(1)}, u32[]{:S(2)}, u32[]{:S(2)}) async-start(bf16[4,64,2048]{2,1,0:T(8,128)(2,1)} %shard_map.126), calls=%async_computation.4 | async-start | bytes 2097152 | tf_op jit(solution)/shard_map/all_to_all | solution.py:452

commit v5 on v4

--- a/solution.py
+++ b/solution.py
@@ -18,13 +18,19 @@
 N_Z = 16
 N_Y = 4
 N_MP = 8
-TILE = 64
+PAIR = 2 * N_Y
+N_PAIRS = N_Z // 2
+ROWS = 32
+COLS = 256
 LIMIT = 48 * 1024 * 1024
 NN = (((1,), (0,)), ((), ()))
 NT = (((1,), (1,)), ((), ()))
 
 Z_GROUPS = [[z * N_Y + y for z in range(N_Z)] for y in range(N_Y)]
-Y_GROUPS = [[z * N_Y + y for y in range(N_Y)] for z in range(N_Z)]
+EVERY_OTHER = [
+    [(z + i) * N_Y + y for z in range(0, N_Z, 2)] for i in range(2) for y in range(N_Y)
+]
+PAIRS = [[k * PAIR + i for i in range(PAIR)] for k in range(N_PAIRS)]
 PLANES = [[z * N_Y * N_MP + i for i in range(N_Y * N_MP)] for z in range(N_Z)]
 
 
@@ -135,15 +141,15 @@
     left = jnp.concatenate(normed, axis=0)
     fetches[3].wait()
     stores = []
-    for z in range(N_Z):
+    for k in range(N_PAIRS):
         part = lax.dot_general(
-            left, up_ref[:, z * HD : (z + 1) * HD], NN, preferred_element_type=F32
+            left, up_ref[:, k * COLS : (k + 1) * COLS], NN, preferred_element_type=F32
         ).astype(BF16)
-        for y in range(N_Y):
-            g_ref[z * N_Y + y] = part[y * TILE : (y + 1) * TILE, :]
-        tiles = pl.ds(z * N_Y, N_Y)
-        stores.append(pltpu.make_async_copy(g_ref.at[tiles], g_any.at[tiles], out_sems.at[z]))
-        stores[z].start()
+        for i in range(PAIR):
+            g_ref[k * PAIR + i] = part[i * ROWS : (i + 1) * ROWS, :]
+        tiles = pl.ds(k * PAIR, PAIR)
+        stores.append(pltpu.make_async_copy(g_ref.at[tiles], g_any.at[tiles], out_sems.at[k]))
+        stores[k].start()
     for store in stores:
         store.wait()
 
@@ -243,11 +249,12 @@
 
 
 def gram_kernel(place_ref, x_ref, small_ref, out_ref, wide):
-    wide[...] = x_ref[...].astype(F32).reshape(REPS * TILE, HD)
+    for e in range(2):
+        wide[e] = x_ref[:, :, e * HD : (e + 1) * HD].astype(F32).reshape(REPS * ROWS, HD)
     total = jnp.zeros((REPS, REPS), F32)
-    for f in range(0, TILE, 2):
+    for f in range(ROWS):
         rows = jnp.concatenate(
-            [wide[pl.ds(f + e, REPS, stride=TILE), :].astype(BF16) for e in range(2)], axis=1
+            [wide[e, pl.ds(f, REPS, stride=ROWS), :].astype(BF16) for e in range(2)], axis=1
         )
         total = total + lax.dot_general(rows, rows, NT, preferred_element_type=F32)
     packed, last = pack_gram(total)
@@ -338,17 +345,17 @@
     for z in range(1, N_Z):
         total = total + in_ref[z].astype(F32)
     gram = unpack_gram(total[0:16], total[16:17])
-    factor[...] = jnp.broadcast_to(path_coefs(gram), (REPS, HD))
-    total = jnp.zeros((TILE, HD), F32)
+    factor[...] = jnp.broadcast_to(path_coefs(gram), (REPS, COLS))
+    total = jnp.zeros((ROWS, COLS), F32)
     for r in range(REPS):
         total = total + factor[r : r + 1, :] * x_ref[r].astype(F32)
     out_ref[...] = jnp.broadcast_to(total.astype(BF16)[None], out_ref.shape)
 
 
 def unfold_kernel(in_ref, out_ref):
-    for z in range(N_Z):
-        out_ref[:, :, z * HD : (z + 1) * HD] = jnp.broadcast_to(
-            in_ref[z][None], (N_Y, TILE, HD)
+    for k in range(N_PAIRS):
+        out_ref[:, :, k * COLS : (k + 1) * COLS] = jnp.broadcast_to(
+            in_ref[k][None], (PAIR, ROWS, COLS)
         )
 
 
@@ -378,13 +385,13 @@
 def forward(big, rows, gain_row):
     (tiles,) = call(
         forward_kernel,
-        [shape((REPS, TILE, HD), BF16)],
+        [shape((REPS, ROWS, COLS), BF16)],
         [*big, *rows, gain_row],
         scratch=[pltpu.VMEM(a.shape, BF16) for a in big]
         + [
-            pltpu.VMEM((REPS, TILE, HD), BF16),
+            pltpu.VMEM((REPS, ROWS, COLS), BF16),
             pltpu.SemaphoreType.DMA((4,)),
-            pltpu.SemaphoreType.DMA((N_Z,)),
+            pltpu.SemaphoreType.DMA((N_PAIRS,)),
         ],
         hbm=(0, 1, 2, 3),
         out_hbm=(0,),
@@ -413,7 +420,7 @@
         gram_kernel,
         [shape((N_Y * N_MP, 32, HD), BF16)],
         [place, stack, small],
-        scratch=[pltpu.VMEM((REPS * TILE, HD), F32)],
+        scratch=[pltpu.VMEM((2, REPS * ROWS, HD), F32)],
         smem=(0,),
         flops=10**9,
     )
@@ -423,9 +430,9 @@
 def combine(packed, stack):
     (tile,) = call(
         combine_kernel,
-        [shape((N_Z, TILE, HD), BF16)],
+        [shape((N_PAIRS, ROWS, COLS), BF16)],
         [packed, stack],
-        scratch=[pltpu.VMEM((REPS, HD), F32)],
+        scratch=[pltpu.VMEM((REPS, COLS), F32)],
         flops=10**8,
     )
     return tile
@@ -447,14 +454,14 @@
     (part,) = call(spread_kernel, [shape((N_Z, 32, HD), BF16)], [part])
     packed = lax.all_to_all(part, "dp", 0, 0, axis_index_groups=Z_GROUPS)
     whole = combine(packed, stack)
-    whole = lax.all_to_all(whole, "dp", 0, 0, axis_index_groups=Z_GROUPS)
-    (whole,) = call(unfold_kernel, [shape((N_Y, TILE, N_Z * HD), BF16)], [whole])
-    whole = lax.all_to_all(whole, "dp", 0, 0, axis_index_groups=Y_GROUPS)
+    whole = lax.all_to_all(whole, "dp", 0, 0, axis_index_groups=EVERY_OTHER)
+    (whole,) = call(unfold_kernel, [shape((PAIR, ROWS, N_PAIRS * COLS), BF16)], [whole])
+    whole = lax.all_to_all(whole, "dp", 0, 0, axis_index_groups=PAIRS)
     gain_final, rate_final = call(
         trees_kernel, [shape((1, HD)), shape((1, HD))], [packed]
     )
     return (
-        whole.reshape(N_Y * TILE, N_Z * HD),
+        whole.reshape(PAIR * ROWS, N_PAIRS * COLS),
         gain_final[0],
         rate_final[0, : HEADS * N_MP],
     )

time: 160 us -> 155 us (0.969)
  blocking collectives: 57.1 us -> 53.3 us
  waiting for transfers between devices: 59.5 us -> 56.7 us
    all_to_all x1, blocking collectives: 22.7 us -> 18.9 us  [per_device(): whole = lax.all_to_all(whole, 'dp', 0, 0, axis_index_groups=EVERY_OTHER)]
    all_to_all x1, waiting for transfers between devices: 12.8 us -> 10.1 us  [per_device(): whole = lax.all_to_all(whole, 'dp', 0, 0, axis_index_groups=PAIRS)]
  transfers between devices with their start and end apart: 2 -> 2, of which waited for: 2 -> 2; matrix products, arithmetic and copies ran while one was open for 0% -> 0% of each run, Pallas kernels for 5% -> 6%
where the time goes in v5:
time: 155 us; the launch traced here: 154 us
  waiting for transfers between devices  56.7 us (37%)
  blocking collectives  53.3 us (34%)
  starting transfers between devices  23.4 us (15%)
  Pallas kernels  18.9 us (12%)
    all_to_all x1, waiting for transfers between devices, per_device(): stack = lax.all_to_all(tiles, 'dp', 0, 0)  46.6 us
    all_to_all x1, blocking collectives, per_device(): whole = lax.all_to_all(whole, 'dp', 0, 0, axis_index_groups=EVERY_OTHER)  18.9 us
    pallas_call x7, Pallas kernels, call(): pl.pallas_call(body, out_shape=outs, in_specs=[pl.BlockSpec(memory_space=...  18.9 us
    all_to_all x1, blocking collectives, per_device(): packed = lax.all_to_all(part, 'dp', 0, 0, axis_index_groups=Z_GROUPS)  18.8 us
    all_to_all x1, starting transfers between devices, per_device(): stack = lax.all_to_all(tiles, 'dp', 0, 0)  18.4 us
    all_to_all x1, blocking collectives, per_device(): part = lax.all_to_all(part, ('dp', 'mp'), 0, 0, axis_index_groups=PLANES)  15.6 us
    all_to_all x1, waiting for transfers between devices, per_device(): whole = lax.all_to_all(whole, 'dp', 0, 0, axis_index_groups=PAIRS)  10.1 us
    all_to_all x1, starting transfers between devices, per_device(): whole = lax.all_to_all(whole, 'dp', 0, 0, axis_index_groups=PAIRS)  5.04 us
  transfers between devices with their start and end apart: 2, of which 2 were waited for; matrix products, arithmetic and copies ran while one was open for 0% of the time, Pallas kernels for 6%

profile of v5, /device:TPU:32, one launch (start us, length us, event | category | flops | bytes accessed | tf_op | source)
XLA Modules:
  0.0 154.5 jit_solution(5192538239485140061)
XLA Ops:
  0.6 5.5 %shard_map.121._ = bf16[64,32,256]{2,1,0:T(8,128)(2,1)} custom-call(bf16[128,128]{1,0:T(8,128)(2,1)} %k_any.3, bf16[128,128]{1,0:T(8,128)(2,1)} %q_any.3, bf16[128,256]{1,0:T(8,128)(2,1)} %v_any.3, bf16[128,2048]{1,0:T(8,128)(2,1)} %up_any.3, f32[2,128]{1,0:T(2,128)} %bitcast.12, f32[2,128]{1,0:T(2,128)} %bitcast.14, f32[1,2]{1,0:T(1,128)} %bitcast.16, ...), custom_call_target="tpu_custom_call" | custom-call | flops 2000000000 | bytes 1706512 | tf_op jit(solution)/shard_map/pallas_call | solution.py:367
  6.1 18.4 %all-to-all-start = ((bf16[64,32,256]{2,1,0:T(8,128)(2,1)}), bf16[64,32,256]{2,1,0:T(8,128)(2,1)S(1)}, u32[]{:S(2)}, u32[]{:S(2)}) async-start(bf16[64,32,256]{2,1,0:T(8,128)(2,1)} %shard_map.121._), calls=%async_computation | async-start | bytes 2097152 | tf_op jit(solution)/shard_map/all_to_all | solution.py:448
  24.5 7.5 %shard_map.122.small_ref = f32[2,128]{1,0:T(2,128)} custom-call(s32[1]{0:T(128)} %bitcast.6.place_ref, bf16[128,128]{1,0:T(8,128)(2,1)} %k_any.3, bf16[128,128]{1,0:T(8,128)(2,1)} %q_any.3, bf16[128,256]{1,0:T(8,128)(2,1)} %v_any.3, bf16[128,2048]{1,0:T(8,128)(2,1)} %up_any.3, bf16[256,2048]{1,0:T(8,128)(2,1)} %weight_any.1, ...), custom_call_target="tpu_custom_call" | custom-call | flops 2000000000 | bytes 2756116 | tf_op jit(solution)/shard_map/pallas_call | solution.py:367
  32.0 0.0 copy-start
  32.0 46.6 %all-to-all-done.x_ref = bf16[64,32,256]{2,1,0:T(8,128)(2,1)S(1)} async-done(((bf16[64,32,256]{2,1,0:T(8,128)(2,1)}), bf16[64,32,256]{2,1,0:T(8,128)(2,1)S(1)}, u32[]{:S(2)}, u32[]{:S(2)}) %all-to-all-start) | async-done | bytes 1048608 | tf_op jit(solution)/shard_map/all_to_all | solution.py:448
  78.7 0.0 copy-done
  78.7 2.0 %shard_map.123 = bf16[32,32,128]{2,1,0:T(8,128)(2,1)S(1)} custom-call(s32[1]{0:T(128)} %bitcast.place_ref, bf16[64,32,256]{2,1,0:T(8,128)(2,1)S(1)} %all-to-all-done.x_ref, f32[2,128]{1,0:T(2,128)S(1)} %copy-done), custom_call_target="tpu_custom_call" | custom-call | flops 1000000000 | bytes 1311748 | tf_op jit(solution)/shard_map/pallas_call | solution.py:367
  80.7 15.6 %all_to_all.25.in_ref = bf16[32,32,128]{2,1,0:T(8,128)(2,1)S(1)} all-to-all(bf16[32,32,128]{2,1,0:T(8,128)(2,1)S(1)} %shard_map.123), channel_id=1, replica_groups={{0,1,2,3,4,5,6,7,8,9,10,11,12,13,14,15,16,17,18,19,20,21,22,23,24,25,26..., dimensions={0} | all-to-all | bytes 524288 | tf_op jit(solution)/shard_map/all_to_all | solution.py:453
  96.3 0.1 shard_map.124
  96.4 18.8 %all_to_all.26.in_ref = bf16[16,32,128]{2,1,0:T(8,128)(2,1)S(1)} all-to-all(bf16[16,32,128]{2,1,0:T(8,128)(2,1)S(1)} %shard_map.124), channel_id=1, replica_groups={{0,32,64,96,128,160,192,224,256,288,320,352,384,416,448,480},{8,40,72,1..., dimensions={0} | all-to-all | bytes 262144 | tf_op jit(solution)/shard_map/all_to_all | solution.py:455
  115.2 1.5 shard_map.125
  116.7 18.9 %all_to_all.27.in_ref = bf16[8,32,256]{2,1,0:T(8,128)(2,1)S(1)} all-to-all(bf16[8,32,256]{2,1,0:T(8,128)(2,1)S(1)} %shard_map.125), channel_id=1, replica_groups={{0,64,128,192,256,320,384,448},{8,72,136,200,264,328,392,456},{16,80,14..., dimensions={0} | all-to-all | bytes 262144 | tf_op jit(solution)/shard_map/all_to_all | solution.py:457
  135.6 1.1 shard_map.126
  136.7 5.0 %all-to-all-start.4 = ((bf16[8,32,2048]{2,1,0:T(8,128)(2,1)}), bf16[8,32,2048]{2,1,0:T(8,128)(2,1)S(1)}, u32[]{:S(2)}, u32[]{:S(2)}) async-start(bf16[8,32,2048]{2,1,0:T(8,128)(2,1)} %shard_map.126), calls=%async_computation.4 | async-start | bytes 2097152 | tf_op jit(solution)/shard_map/all_to_all | solution.py:459
  141.7 1.2 shard_map.127
  142.9 0.5 slice_bitcast_fusion
  143.4 10.1 %all-to-all-done.4 = bf16[8,32,2048]{2,1,0:T(8,128)(2,1)S(1)} async-done(((bf16[8,32,2048]{2,1,0:T(8,128)(2,1)}), bf16[8,32,2048]{2,1,0:T(8,128)(2,1)S(1)}, u32[]{:S(2)}, u32[]{:S(2)}) %all-to-all-start.4) | async-done | bytes 1048608 | tf_op jit(solution)/shard_map/all_to_all | solution.py:459
  153.5 1.0 copy.14
Async XLA Ops:
  6.1 72.5 %all-to-all-start = ((bf16[64,32,256]{2,1,0:T(8,128)(2,1)}), bf16[64,32,256]{2,1,0:T(8,128)(2,1)S(1)}, u32[]{:S(2)}, u32[]{:S(2)}) async-start(bf16[64,32,256]{2,1,0:T(8,128)(2,1)} %shard_map.121._), calls=%async_computation | async-start | bytes 2097152 | tf_op jit(solution)/shard_map/all_to_all | solution.py:448
  32.0 46.6 %copy-start = (f32[2,128]{1,0:T(2,128)S(1)}, f32[2,128]{1,0:T(2,128)}, u32[]{:S(2)}) copy-start(f32[2,128]{1,0:T(2,128)} %shard_map.122.small_ref) | copy-start | bytes 3076
  136.7 16.9 %all-to-all-start.4 = ((bf16[8,32,2048]{2,1,0:T(8,128)(2,1)}), bf16[8,32,2048]{2,1,0:T(8,128)(2,1)S(1)}, u32[]{:S(2)}, u32[]{:S(2)}) async-start(bf16[8,32,2048]{2,1,0:T(8,128)(2,1)} %shard_map.126), calls=%async_computation.4 | async-start | bytes 2097152 | tf_op jit(solution)/shard_map/all_to_all | solution.py:459

commit v6 on v5

--- a/solution.py
+++ b/solution.py
@@ -22,6 +22,7 @@
 N_PAIRS = N_Z // 2
 ROWS = 32
 COLS = 256
+PITCH = 36
 LIMIT = 48 * 1024 * 1024
 NN = (((1,), (0,)), ((), ()))
 NT = (((1,), (1,)), ((), ()))
@@ -250,11 +251,12 @@
 
 def gram_kernel(place_ref, x_ref, small_ref, out_ref, wide):
     for e in range(2):
-        wide[e] = x_ref[:, :, e * HD : (e + 1) * HD].astype(F32).reshape(REPS * ROWS, HD)
+        for r in range(REPS):
+            wide[e, pl.ds(r * PITCH, ROWS), :] = x_ref[r, :, e * HD : (e + 1) * HD].astype(F32)
     total = jnp.zeros((REPS, REPS), F32)
     for f in range(ROWS):
         rows = jnp.concatenate(
-            [wide[e, pl.ds(f, REPS, stride=ROWS), :].astype(BF16) for e in range(2)], axis=1
+            [wide[e, pl.ds(f, REPS, stride=PITCH), :].astype(BF16) for e in range(2)], axis=1
         )
         total = total + lax.dot_general(rows, rows, NT, preferred_element_type=F32)
     packed, last = pack_gram(total)
@@ -352,11 +354,25 @@
     out_ref[...] = jnp.broadcast_to(total.astype(BF16)[None], out_ref.shape)
 
 
-def unfold_kernel(in_ref, out_ref):
+def unfold_kernel(in_ref, out_any, line_ref, sems):
     for k in range(N_PAIRS):
-        out_ref[:, :, k * COLS : (k + 1) * COLS] = jnp.broadcast_to(
-            in_ref[k][None], (PAIR, ROWS, COLS)
-        )
+        line_ref[:, k * COLS : (k + 1) * COLS] = in_ref[k]
+    stores = [pltpu.make_async_copy(line_ref, out_any.at[i], sems.at[i]) for i in range(PAIR)]
+    for store in stores:
+        store.start()
+    for store in stores:
+        store.wait()
+
+
+def unfold(tiles):
+    (out,) = call(
+        unfold_kernel,
+        [shape((PAIR, ROWS, N_PAIRS * COLS), BF16)],
+        [tiles],
+        scratch=[pltpu.VMEM((ROWS, N_PAIRS * COLS), BF16), pltpu.SemaphoreType.DMA((PAIR,))],
+        out_hbm=(0,),
+    )
+    return out
 
 
 def call(body, outs, ops, scratch=(), smem=(), hbm=(), out_hbm=(), flops=0, limit=LIMIT):
@@ -420,7 +436,7 @@
         gram_kernel,
         [shape((N_Y * N_MP, 32, HD), BF16)],
         [place, stack, small],
-        scratch=[pltpu.VMEM((2, REPS * ROWS, HD), F32)],
+        scratch=[pltpu.VMEM((2, REPS * PITCH + 64, HD), F32)],
         smem=(0,),
         flops=10**9,
     )
@@ -455,7 +471,7 @@
     packed = lax.all_to_all(part, "dp", 0, 0, axis_index_groups=Z_GROUPS)
     whole = combine(packed, stack)
     whole = lax.all_to_all(whole, "dp", 0, 0, axis_index_groups=EVERY_OTHER)
-    (whole,) = call(unfold_kernel, [shape((PAIR, ROWS, N_PAIRS * COLS), BF16)], [whole])
+    whole = unfold(whole)
     whole = lax.all_to_all(whole, "dp", 0, 0, axis_index_groups=PAIRS)
     gain_final, rate_final = call(
         trees_kernel, [shape((1, HD)), shape((1, HD))], [packed]

time: 155 us -> 154 us (level)
  no operation moved by 1% of the time
where the time goes in v6:
time: 154 us; the launch traced here: 153 us
  waiting for transfers between devices  56.7 us (37%)
  blocking collectives  53.3 us (35%)
  starting transfers between devices  23.4 us (15%)
  Pallas kernels  17.8 us (12%)
    all_to_all x1, waiting for transfers between devices, per_device(): stack = lax.all_to_all(tiles, 'dp', 0, 0)  46.6 us
    all_to_all x1, blocking collectives, per_device(): whole = lax.all_to_all(whole, 'dp', 0, 0, axis_index_groups=EVERY_OTHER)  18.9 us
    all_to_all x1, blocking collectives, per_device(): packed = lax.all_to_all(part, 'dp', 0, 0, axis_index_groups=Z_GROUPS)  18.8 us
    all_to_all x1, starting transfers between devices, per_device(): stack = lax.all_to_all(tiles, 'dp', 0, 0)  18.4 us
    pallas_call x7, Pallas kernels, call(): pl.pallas_call(body, out_shape=outs, in_specs=[pl.BlockSpec(memory_space=...  17.8 us
    all_to_all x1, blocking collectives, per_device(): part = lax.all_to_all(part, ('dp', 'mp'), 0, 0, axis_index_groups=PLANES)  15.6 us
    all_to_all x1, waiting for transfers between devices, per_device(): whole = lax.all_to_all(whole, 'dp', 0, 0, axis_index_groups=PAIRS)  10.1 us
    all_to_all x1, starting transfers between devices, per_device(): whole = lax.all_to_all(whole, 'dp', 0, 0, axis_index_groups=PAIRS)  5.05 us
  transfers between devices with their start and end apart: 2, of which 2 were waited for; matrix products, arithmetic and copies ran while one was open for 0% of the time, Pallas kernels for 6%

profile of v6, /device:TPU:32, one launch (start us, length us, event | category | flops | bytes accessed | tf_op | source)
XLA Modules:
  0.0 153.4 jit_solution(10326873052224547303)
XLA Ops:
  0.6 5.5 %shard_map.121._ = bf16[64,32,256]{2,1,0:T(8,128)(2,1)} custom-call(bf16[128,128]{1,0:T(8,128)(2,1)} %k_any.3, bf16[128,128]{1,0:T(8,128)(2,1)} %q_any.3, bf16[128,256]{1,0:T(8,128)(2,1)} %v_any.3, bf16[128,2048]{1,0:T(8,128)(2,1)} %up_any.3, f32[2,128]{1,0:T(2,128)} %bitcast.12, f32[2,128]{1,0:T(2,128)} %bitcast.14, f32[1,2]{1,0:T(1,128)} %bitcast.16, ...), custom_call_target="tpu_custom_call" | custom-call | flops 2000000000 | bytes 1706512 | tf_op jit(solution)/shard_map/pallas_call | solution.py:383
  6.1 18.4 %all-to-all-start = ((bf16[64,32,256]{2,1,0:T(8,128)(2,1)}), bf16[64,32,256]{2,1,0:T(8,128)(2,1)S(1)}, u32[]{:S(2)}, u32[]{:S(2)}) async-start(bf16[64,32,256]{2,1,0:T(8,128)(2,1)} %shard_map.121._), calls=%async_computation | async-start | bytes 2097152 | tf_op jit(solution)/shard_map/all_to_all | solution.py:464
  24.5 7.5 %shard_map.122.small_ref = f32[2,128]{1,0:T(2,128)} custom-call(s32[1]{0:T(128)} %bitcast.6.place_ref, bf16[128,128]{1,0:T(8,128)(2,1)} %k_any.3, bf16[128,128]{1,0:T(8,128)(2,1)} %q_any.3, bf16[128,256]{1,0:T(8,128)(2,1)} %v_any.3, bf16[128,2048]{1,0:T(8,128)(2,1)} %up_any.3, bf16[256,2048]{1,0:T(8,128)(2,1)} %weight_any.1, ...), custom_call_target="tpu_custom_call" | custom-call | flops 2000000000 | bytes 2756116 | tf_op jit(solution)/shard_map/pallas_call | solution.py:383
  32.0 0.0 copy-start
  32.0 46.6 %all-to-all-done.x_ref = bf16[64,32,256]{2,1,0:T(8,128)(2,1)S(1)} async-done(((bf16[64,32,256]{2,1,0:T(8,128)(2,1)}), bf16[64,32,256]{2,1,0:T(8,128)(2,1)S(1)}, u32[]{:S(2)}, u32[]{:S(2)}) %all-to-all-start) | async-done | bytes 1048608 | tf_op jit(solution)/shard_map/all_to_all | solution.py:464
  78.7 0.0 copy-done
  78.7 1.0 shard_map.123
  79.6 15.6 %all_to_all.25.in_ref = bf16[32,32,128]{2,1,0:T(8,128)(2,1)S(1)} all-to-all(bf16[32,32,128]{2,1,0:T(8,128)(2,1)S(1)} %shard_map.123), channel_id=1, replica_groups={{0,1,2,3,4,5,6,7,8,9,10,11,12,13,14,15,16,17,18,19,20,21,22,23,24,25,26..., dimensions={0} | all-to-all | bytes 524288 | tf_op jit(solution)/shard_map/all_to_all | solution.py:469
  95.3 0.1 shard_map.124
  95.4 18.8 %all_to_all.26.in_ref = bf16[16,32,128]{2,1,0:T(8,128)(2,1)S(1)} all-to-all(bf16[16,32,128]{2,1,0:T(8,128)(2,1)S(1)} %shard_map.124), channel_id=1, replica_groups={{0,32,64,96,128,160,192,224,256,288,320,352,384,416,448,480},{8,40,72,1..., dimensions={0} | all-to-all | bytes 262144 | tf_op jit(solution)/shard_map/all_to_all | solution.py:471
  114.2 1.5 shard_map.125
  115.7 18.9 %all_to_all.27.in_ref = bf16[8,32,256]{2,1,0:T(8,128)(2,1)S(1)} all-to-all(bf16[8,32,256]{2,1,0:T(8,128)(2,1)S(1)} %shard_map.125), channel_id=1, replica_groups={{0,64,128,192,256,320,384,448},{8,72,136,200,264,328,392,456},{16,80,14..., dimensions={0} | all-to-all | bytes 262144 | tf_op jit(solution)/shard_map/all_to_all | solution.py:473
  134.6 1.0 shard_map.126
  135.6 5.1 %all-to-all-start.4 = ((bf16[8,32,2048]{2,1,0:T(8,128)(2,1)}), bf16[8,32,2048]{2,1,0:T(8,128)(2,1)S(1)}, u32[]{:S(2)}, u32[]{:S(2)}) async-start(bf16[8,32,2048]{2,1,0:T(8,128)(2,1)} %shard_map.126), calls=%async_computation.4 | async-start | bytes 2097152 | tf_op jit(solution)/shard_map/all_to_all | solution.py:475
  140.6 1.2 shard_map.127
  141.9 0.5 slice_bitcast_fusion
  142.4 10.1 %all-to-all-done.4 = bf16[8,32,2048]{2,1,0:T(8,128)(2,1)S(1)} async-done(((bf16[8,32,2048]{2,1,0:T(8,128)(2,1)}), bf16[8,32,2048]{2,1,0:T(8,128)(2,1)S(1)}, u32[]{:S(2)}, u32[]{:S(2)}) %all-to-all-start.4) | async-done | bytes 1048608 | tf_op jit(solution)/shard_map/all_to_all | solution.py:475
  152.5 1.0 copy.14
Async XLA Ops:
  6.1 72.5 %all-to-all-start = ((bf16[64,32,256]{2,1,0:T(8,128)(2,1)}), bf16[64,32,256]{2,1,0:T(8,128)(2,1)S(1)}, u32[]{:S(2)}, u32[]{:S(2)}) async-start(bf16[64,32,256]{2,1,0:T(8,128)(2,1)} %shard_map.121._), calls=%async_computation | async-start | bytes 2097152 | tf_op jit(solution)/shard_map/all_to_all | solution.py:464
  32.0 46.6 %copy-start = (f32[2,128]{1,0:T(2,128)S(1)}, f32[2,128]{1,0:T(2,128)}, u32[]{:S(2)}) copy-start(f32[2,128]{1,0:T(2,128)} %shard_map.122.small_ref) | copy-start | bytes 3076
  135.6 16.9 %all-to-all-start.4 = ((bf16[8,32,2048]{2,1,0:T(8,128)(2,1)}), bf16[8,32,2048]{2,1,0:T(8,128)(2,1)S(1)}, u32[]{:S(2)}, u32[]{:S(2)}) async-start(bf16[8,32,2048]{2,1,0:T(8,128)(2,1)} %shard_map.126), calls=%async_computation.4 | async-start | bytes 2097152 | tf_op jit(solution)/shard_map/all_to_all | solution.py:475

commit v7 on v6

--- a/solution.py
+++ b/solution.py
@@ -28,8 +28,11 @@
 NT = (((1,), (1,)), ((), ()))
 
 Z_GROUPS = [[z * N_Y + y for z in range(N_Z)] for y in range(N_Y)]
+Z_ORDER = [int(f"{z:04b}"[::-1], 2) for z in range(N_Z)]
+ORDER = [z * N_Y + y for z in Z_ORDER for y in range(N_Y)]
+K_ORDER = [0, 4, 2, 6, 1, 5, 3, 7]
 EVERY_OTHER = [
-    [(z + i) * N_Y + y for z in range(0, N_Z, 2)] for i in range(2) for y in range(N_Y)
+    [(2 * k + i) * N_Y + y for k in K_ORDER] for i in range(2) for y in range(N_Y)
 ]
 PAIRS = [[k * PAIR + i for i in range(PAIR)] for k in range(N_PAIRS)]
 PLANES = [[z * N_Y * N_MP + i for i in range(N_Y * N_MP)] for z in range(N_Z)]
@@ -146,11 +149,14 @@
         part = lax.dot_general(
             left, up_ref[:, k * COLS : (k + 1) * COLS], NN, preferred_element_type=F32
         ).astype(BF16)
-        for i in range(PAIR):
-            g_ref[k * PAIR + i] = part[i * ROWS : (i + 1) * ROWS, :]
-        tiles = pl.ds(k * PAIR, PAIR)
-        stores.append(pltpu.make_async_copy(g_ref.at[tiles], g_any.at[tiles], out_sems.at[k]))
-        stores[k].start()
+        for i in range(2):
+            z = 2 * k + i
+            slot = Z_ORDER.index(z) * N_Y
+            for y in range(N_Y):
+                g_ref[slot + y] = part[(i * N_Y + y) * ROWS : (i * N_Y + y + 1) * ROWS, :]
+            tiles = pl.ds(slot, N_Y)
+            stores.append(pltpu.make_async_copy(g_ref.at[tiles], g_any.at[tiles], out_sems.at[z]))
+            stores[z].start()
     for store in stores:
         store.wait()
 
@@ -252,7 +258,7 @@
 def gram_kernel(place_ref, x_ref, small_ref, out_ref, wide):
     for e in range(2):
         for r in range(REPS):
-            wide[e, pl.ds(r * PITCH, ROWS), :] = x_ref[r, :, e * HD : (e + 1) * HD].astype(F32)
+            wide[e, pl.ds(ORDER[r] * PITCH, ROWS), :] = x_ref[r, :, e * HD : (e + 1) * HD].astype(F32)
     total = jnp.zeros((REPS, REPS), F32)
     for f in range(ROWS):
         rows = jnp.concatenate(
@@ -350,13 +356,13 @@
     factor[...] = jnp.broadcast_to(path_coefs(gram), (REPS, COLS))
     total = jnp.zeros((ROWS, COLS), F32)
     for r in range(REPS):
-        total = total + factor[r : r + 1, :] * x_ref[r].astype(F32)
+        total = total + factor[ORDER[r] : ORDER[r] + 1, :] * x_ref[r].astype(F32)
     out_ref[...] = jnp.broadcast_to(total.astype(BF16)[None], out_ref.shape)
 
 
 def unfold_kernel(in_ref, out_any, line_ref, sems):
-    for k in range(N_PAIRS):
-        line_ref[:, k * COLS : (k + 1) * COLS] = in_ref[k]
+    for i, k in enumerate(K_ORDER):
+        line_ref[:, k * COLS : (k + 1) * COLS] = in_ref[i]
     stores = [pltpu.make_async_copy(line_ref, out_any.at[i], sems.at[i]) for i in range(PAIR)]
     for store in stores:
         store.start()
@@ -407,7 +413,7 @@
         + [
             pltpu.VMEM((REPS, ROWS, COLS), BF16),
             pltpu.SemaphoreType.DMA((4,)),
-            pltpu.SemaphoreType.DMA((N_PAIRS,)),
+            pltpu.SemaphoreType.DMA((N_Z,)),
         ],
         hbm=(0, 1, 2, 3),
         out_hbm=(0,),
@@ -461,7 +467,7 @@
     big = (key_raw, query_raw, values, upstream)
     rows = (decay_input.T, beta_input.T, log_rate[None, :], step_bias[None, :])
     tiles = forward(big, rows, gain_row)
-    stack = lax.all_to_all(tiles, "dp", 0, 0)
+    stack = lax.all_to_all(tiles, "dp", 0, 0, axis_index_groups=[ORDER])
     place = lax.axis_index("mp").astype(jnp.int32)[None]
     small = backward(place, (*big, out_weight), tiles, rows, gain_row)
     place = (lax.axis_index("dp") % N_Y).astype(jnp.int32)[None]

time: 154 us -> 152 us (0.987)
  the two profiles are of different devices: /device:TPU:32 before, /device:TPU:64 now
where the time goes in v7:
time: 152 us; the launch traced here: 151 us
  waiting for transfers between devices  57.7 us (38%)
  blocking collectives  52 us (34%)
  starting transfers between devices  21.5 us (14%)
  Pallas kernels  17.8 us (12%)
    all_to_all x1, waiting for transfers between devices, per_device(): stack = lax.all_to_all(tiles, 'dp', 0, 0, axis_index_groups=[ORDER])  46.5 us
    all_to_all x1, blocking collectives, per_device(): packed = lax.all_to_all(part, 'dp', 0, 0, axis_index_groups=Z_GROUPS)  19.8 us
    all_to_all x1, blocking collectives, per_device(): whole = lax.all_to_all(whole, 'dp', 0, 0, axis_index_groups=EVERY_OTHER)  18.3 us
    all_to_all x1, starting transfers between devices, per_device(): stack = lax.all_to_all(tiles, 'dp', 0, 0, axis_index_groups=[ORDER])  17.9 us
    pallas_call x7, Pallas kernels, call(): pl.pallas_call(body, out_shape=outs, in_specs=[pl.BlockSpec(memory_space=...  17.8 us
    all_to_all x1, blocking collectives, per_device(): part = lax.all_to_all(part, ('dp', 'mp'), 0, 0, axis_index_groups=PLANES)  13.9 us
    all_to_all x1, waiting for transfers between devices, per_device(): whole = lax.all_to_all(whole, 'dp', 0, 0, axis_index_groups=PAIRS)  11.2 us
    all_to_all x1, starting transfers between devices, per_device(): whole = lax.all_to_all(whole, 'dp', 0, 0, axis_index_groups=PAIRS)  3.57 us
  transfers between devices with their start and end apart: 2, of which 2 were waited for; matrix products, arithmetic and copies ran while one was open for 0% of the time, Pallas kernels for 6%

profile of v7, /device:TPU:64, one launch (start us, length us, event | category | flops | bytes accessed | tf_op | source)
XLA Modules:
  0.0 151.3 jit_solution(7170742152591642195)
XLA Ops:
  0.6 5.5 %shard_map.121._ = bf16[64,32,256]{2,1,0:T(8,128)(2,1)} custom-call(bf16[128,128]{1,0:T(8,128)(2,1)} %k_any.3, bf16[128,128]{1,0:T(8,128)(2,1)} %q_any.3, bf16[128,256]{1,0:T(8,128)(2,1)} %v_any.3, bf16[128,2048]{1,0:T(8,128)(2,1)} %up_any.3, f32[2,128]{1,0:T(2,128)} %bitcast.12, f32[2,128]{1,0:T(2,128)} %bitcast.14, f32[1,2]{1,0:T(1,128)} %bitcast.16, ...), custom_call_target="tpu_custom_call" | custom-call | flops 2000000000 | bytes 1706512 | tf_op jit(solution)/shard_map/pallas_call | solution.py:389
  6.2 17.9 %all-to-all-start = ((bf16[64,32,256]{2,1,0:T(8,128)(2,1)}), bf16[64,32,256]{2,1,0:T(8,128)(2,1)S(1)}, u32[]{:S(2)}, u32[]{:S(2)}) async-start(bf16[64,32,256]{2,1,0:T(8,128)(2,1)} %shard_map.121._), calls=%async_computation | async-start | bytes 2097152 | tf_op jit(solution)/shard_map/all_to_all | solution.py:470
  24.1 7.5 %shard_map.122.small_ref = f32[2,128]{1,0:T(2,128)} custom-call(s32[1]{0:T(128)} %bitcast.6.place_ref, bf16[128,128]{1,0:T(8,128)(2,1)} %k_any.3, bf16[128,128]{1,0:T(8,128)(2,1)} %q_any.3, bf16[128,256]{1,0:T(8,128)(2,1)} %v_any.3, bf16[128,2048]{1,0:T(8,128)(2,1)} %up_any.3, bf16[256,2048]{1,0:T(8,128)(2,1)} %weight_any.1, ...), custom_call_target="tpu_custom_call" | custom-call | flops 2000000000 | bytes 2756116 | tf_op jit(solution)/shard_map/pallas_call | solution.py:389
  31.6 0.0 copy-start
  31.6 46.5 %all-to-all-done.x_ref = bf16[64,32,256]{2,1,0:T(8,128)(2,1)S(1)} async-done(((bf16[64,32,256]{2,1,0:T(8,128)(2,1)}), bf16[64,32,256]{2,1,0:T(8,128)(2,1)S(1)}, u32[]{:S(2)}, u32[]{:S(2)}) %all-to-all-start) | async-done | bytes 1048608 | tf_op jit(solution)/shard_map/all_to_all | solution.py:470
  78.1 0.0 copy-done
  78.1 1.0 shard_map.123
  79.1 13.9 %all_to_all.25.in_ref = bf16[32,32,128]{2,1,0:T(8,128)(2,1)S(1)} all-to-all(bf16[32,32,128]{2,1,0:T(8,128)(2,1)S(1)} %shard_map.123), channel_id=1, replica_groups={{0,1,2,3,4,5,6,7,8,9,10,11,12,13,14,15,16,17,18,19,20,21,22,23,24,25,26..., dimensions={0} | all-to-all | bytes 524288 | tf_op jit(solution)/shard_map/all_to_all | solution.py:475
  93.0 0.1 shard_map.124
  93.1 19.8 %all_to_all.26.in_ref = bf16[16,32,128]{2,1,0:T(8,128)(2,1)S(1)} all-to-all(bf16[16,32,128]{2,1,0:T(8,128)(2,1)S(1)} %shard_map.124), channel_id=1, replica_groups={{0,32,64,96,128,160,192,224,256,288,320,352,384,416,448,480},{8,40,72,1..., dimensions={0} | all-to-all | bytes 262144 | tf_op jit(solution)/shard_map/all_to_all | solution.py:477
  112.9 1.5 shard_map.125
  114.4 18.3 %all_to_all.27.in_ref = bf16[8,32,256]{2,1,0:T(8,128)(2,1)S(1)} all-to-all(bf16[8,32,256]{2,1,0:T(8,128)(2,1)S(1)} %shard_map.125), channel_id=1, replica_groups={{0,256,128,384,64,320,192,448},{8,264,136,392,72,328,200,456},{16,272,1..., dimensions={0} | all-to-all | bytes 262144 | tf_op jit(solution)/shard_map/all_to_all | solution.py:479
  132.7 1.0 shard_map.126
  133.7 3.6 %all-to-all-start.4 = ((bf16[8,32,2048]{2,1,0:T(8,128)(2,1)}), bf16[8,32,2048]{2,1,0:T(8,128)(2,1)S(1)}, u32[]{:S(2)}, u32[]{:S(2)}) async-start(bf16[8,32,2048]{2,1,0:T(8,128)(2,1)} %shard_map.126), calls=%async_computation.4 | async-start | bytes 2097152 | tf_op jit(solution)/shard_map/all_to_all | solution.py:481
  137.3 1.2 shard_map.127
  138.5 0.5 slice_bitcast_fusion
  139.0 11.2 %all-to-all-done.4 = bf16[8,32,2048]{2,1,0:T(8,128)(2,1)S(1)} async-done(((bf16[8,32,2048]{2,1,0:T(8,128)(2,1)}), bf16[8,32,2048]{2,1,0:T(8,128)(2,1)S(1)}, u32[]{:S(2)}, u32[]{:S(2)}) %all-to-all-start.4) | async-done | bytes 1048608 | tf_op jit(solution)/shard_map/all_to_all | solution.py:481
  150.3 1.0 copy.14
Async XLA Ops:
  6.2 72.0 %all-to-all-start = ((bf16[64,32,256]{2,1,0:T(8,128)(2,1)}), bf16[64,32,256]{2,1,0:T(8,128)(2,1)S(1)}, u32[]{:S(2)}, u32[]{:S(2)}) async-start(bf16[64,32,256]{2,1,0:T(8,128)(2,1)} %shard_map.121._), calls=%async_computation | async-start | bytes 2097152 | tf_op jit(solution)/shard_map/all_to_all | solution.py:470
  31.6 46.5 %copy-start = (f32[2,128]{1,0:T(2,128)S(1)}, f32[2,128]{1,0:T(2,128)}, u32[]{:S(2)}) copy-start(f32[2,128]{1,0:T(2,128)} %shard_map.122.small_ref) | copy-start | bytes 3076
  133.7 16.6 %all-to-all-start.4 = ((bf16[8,32,2048]{2,1,0:T(8,128)(2,1)}), bf16[8,32,2048]{2,1,0:T(8,128)(2,1)S(1)}, u32[]{:S(2)}, u32[]{:S(2)}) async-start(bf16[8,32,2048]{2,1,0:T(8,128)(2,1)} %shard_map.126), calls=%async_computation.4 | async-start | bytes 2097152 | tf_op jit(solution)/shard_map/all_to_all | solution.py:481
